TPU v7x, 768 devices: a whole 4x8x12 slice. The times are simulated.
768 devices in a mesh: comp: 8 (over y), tile: 96 (over x, z, core).
Axes of the slice: x: 4, y: 8, z: 12, core: 2. Of those that a mesh axis runs over, the one named last changes fastest.
Arguments:
- atm_flux: bfloat16 [8, 96, 8, 1024], P('comp', 'tile'), may hold values from -6 to 6
- intersection_weight: bfloat16 [8, 96, 8, 12, 128, 128], P('comp', 'tile'), may hold values from 0 to 0.099609375
- src_block: int32 [8, 96, 8, 12], P('comp', 'tile'), may hold values from 0 to 7
- dst_block: int32 [8, 96, 8, 12], P('comp', 'tile'), may hold values from 0 to 7
- intersection_count: int32 [8, 96, 8, 12], P('comp', 'tile'), may hold values from 0 to 128, as said below
- temp: float32 [8, 96, 48, 1024], P('comp', 'tile'), may hold values from -6 to 6
- kappa: float32 [8, 96, 47, 1024], P('comp', 'tile'), may hold values from 0.02 to 0.3
- ssh: float32 [8, 96, 1024], P('comp', 'tile'), may hold values from -6 to 6
- nbr_offset: int32 [8, 96, 6, 1024], P('comp', 'tile'), may hold values from -64 to 64, as said below
- coupler_perm: int32 [8, 96, 1024], P('comp', 'tile'), may hold values from 0 to 1023, each once within a row
Outputs:
- temp_mixed: float32 [8, 96, 48, 1024], P('comp', 'tile')
- ssh_final: float32 [8, 96, 1024], P('comp', 'tile')
- coupler_state: float32 [8, 96, 3, 1024], P('comp', 'tile')
Inputs may be any that keep to these rules, and one draw needn't show every extreme that they name: `src_block`: an atmosphere block of the sending device. `dst_block`: an ocean block of the receiving device; some blocks take many slots. `intersection_count`: 0 marks an empty slot; every device has a slot that uses all rows. `nbr_offset`: never 0; both ends are reached on every device. `coupler_perm`: a permutation of each device's cells.
All inputs are finite; a program needn't handle non-finite values.
Results may differ from a plain program's by a relative error of at most 0.00085.
Values sent between devices are 32-bit elements; how exact they have to be, the bound alone decides.
No kernel may reach another device: no remote copies, remote signals or barrier semaphores. Data moves between devices by JAX's collectives and lax.ppermute only.
A program may use at most 32 MiB of HBM per device.

v0:
```python
import jax
import jax.numpy as jnp
from jax import lax
from jax.sharding import PartitionSpec as P

W = 64
SUB = 8
MIX = 4


heat_gain = 0.5
shortwave_gain = 0.5
wind_mixing = 0.15
relax_rate = 0.5
fresh_gain = 0.5


def extended_2(block, sides, width):
    for axis, dim in sides:
        count = lax.axis_size(axis)
        forward = [(i, i + 1) for i in range(count - 1)]
        forward.append((count - 1, 0))
        backward = [(target, source) for source, target in forward]
        low = lax.ppermute(
            lax.slice_in_dim(block, block.shape[dim] - width, None, axis=dim), axis, forward
        )
        high = lax.ppermute(lax.slice_in_dim(block, 0, width, axis=dim), axis, backward)
        block = jnp.concatenate([low, block, high], axis=dim)
    return block


def column_update(temp, kappa, forcing):
    levels = jnp.arange(temp.shape[0]).astype(jnp.float32)
    shallow = jnp.exp(-levels / 4.0) - jnp.exp(-(levels + 1.0) / 4.0)
    heated = temp + shortwave_gain * forcing[1:2, :] * shallow[:, None]
    top = heat_gain * (forcing[0, :] + forcing[7, :])
    heated = heated.at[0, :].add(top)
    wind = jnp.sqrt(forcing[2, :] * forcing[2, :] + forcing[3, :] * forcing[3, :])
    decay = jnp.exp(-levels[: temp.shape[0] - 1] / 4.0)
    keff = kappa + wind_mixing * jnp.tanh(wind)[None, :] * decay[:, None]
    for sweep in range(MIX):
        flow = keff * (heated[1:, :] - heated[:-1, :])
        zero = jnp.zeros_like(flow[:1, :])
        heated = (
            heated + jnp.concatenate([flow, zero], axis=0) - jnp.concatenate([zero, flow], axis=0)
        )
    return heated


def neighbour_tiles(offsets, width):
    length = offsets.shape[1]
    local = jnp.arange(length, dtype=jnp.int32) % width + width
    targets = (local[None, :] + offsets).reshape(6, length // width, width)
    window = jnp.arange(3 * width, dtype=jnp.int32)
    tiles = jnp.zeros((length // width, width, 3 * width), jnp.float32)
    for which in range(6):
        tiles = tiles + (targets[which][:, :, None] == window[None, None, :]).astype(jnp.float32)
    return tiles


def neighbour_mean(values, tiles, width):
    rows_of = values.reshape(-1, width)
    windows = jnp.concatenate([rows_of[:-2], rows_of[1:-1], rows_of[2:]], axis=1)
    summed = jnp.einsum("bij,bj->bi", tiles, windows, precision=lax.Precision.HIGHEST)
    return summed.reshape(-1) / 6.0


def per_device(
    atm_flux,
    intersection_weight,
    src_block,
    dst_block,
    intersection_count,
    temp,
    kappa,
    ssh,
    nbr_offset,
    coupler_perm,
):
    groups = lax.axis_size("comp")
    fields = atm_flux.shape[2]
    columns = atm_flux.shape[3]
    slots = intersection_weight.shape[3]
    block_in = intersection_weight.shape[4]
    block_out = intersection_weight.shape[5]
    cells = temp.shape[3]
    blocks_out = cells // block_out
    total_slots = groups * slots
    flux = atm_flux[0, 0].reshape(fields, columns // block_in, block_in).transpose(1, 0, 2)
    picked = flux[src_block[0, 0].reshape(-1)]
    rows = jnp.arange(block_in, dtype=jnp.int32)
    keep = (rows[None, :] < intersection_count[0, 0].reshape(-1)[:, None]).astype(picked.dtype)
    picked = picked * keep[:, None, :]
    weights = intersection_weight[0, 0].reshape(total_slots, block_in, block_out)
    terms = jnp.einsum("mnr,mro->mno", picked, weights, preferred_element_type=jnp.float32)
    terms = terms.reshape(groups, slots, fields, block_out)
    block_ids = jnp.arange(blocks_out, dtype=jnp.int32)
    arrived = lax.all_to_all(terms, "comp", split_axis=0, concat_axis=0, tiled=True)
    targets = dst_block[0, 0].reshape(total_slots)
    onehot = (block_ids[:, None] == targets[None, :]).astype(jnp.float32)
    gathered = jnp.dot(
        onehot, arrived.reshape(total_slots, fields * block_out), precision=lax.Precision.HIGHEST
    )
    forcing = (
        gathered.reshape(blocks_out, fields, block_out).transpose(1, 0, 2).reshape(fields, cells)
    )
    temp_mixed = column_update(temp[0, 0], kappa[0, 0], forcing)
    fresh = forcing[5] - forcing[4] + forcing[6]
    height = ssh[0, 0]
    tiles = neighbour_tiles(nbr_offset[0, 0], W)
    for step in range(SUB):
        extended = extended_2(height, (("tile", 0),), W)
        average = neighbour_mean(extended, tiles, W)
        height = height + relax_rate * (average - height) + fresh_gain * fresh / SUB
    state = jnp.stack([temp_mixed[0], temp_mixed[1], height], axis=0)
    permuted = state[:, coupler_perm[0, 0]].reshape(3, groups, cells // groups)
    relaid = lax.all_to_all(permuted, "comp", split_axis=1, concat_axis=1, tiled=True)
    coupler_state = relaid.reshape(3, cells)
    return (temp_mixed[None, None], height[None, None], coupler_state[None, None])


def solution(mesh):
    return jax.shard_map(
        per_device,
        mesh=mesh,
        in_specs=(
            P("comp", "tile", None, None),
            P("comp", "tile", None, None, None, None),
            P("comp", "tile", None, None),
            P("comp", "tile", None, None),
            P("comp", "tile", None, None),
            P("comp", "tile", None, None),
            P("comp", "tile", None, None),
            P("comp", "tile", None),
            P("comp", "tile", None, None),
            P("comp", "tile", None),
        ),
        out_specs=(
            P("comp", "tile", None, None),
            P("comp", "tile", None),
            P("comp", "tile", None, None),
        ),
        check_vma=False,
    )
```

profile of v0, /device:TPU:8, one launch (start us, length us, event | category | flops | bytes accessed | tf_op | source)
XLA Modules:
  0.0 174.4 jit_solution(13517240449333865024)
XLA Ops:
  1.6 2.0 %collective-permute-start = (f32[64]{0:T(128)S(1)}, f32[64]{0:T(128)S(1)}, u32[]{:S(2)}, u32[]{:S(2)}) collective-permute-start(f32[64]{0:T(128)S(1)} %get-tuple-element.77), channel_id=1, source_target_pairs={{0,1},{1,2},{2,3},{3,4},{4,5},{5,6},{6,7},{7,8},{8,9},{9,10},{10,1... | collective-permute-start | bytes 776 | tf_op jit(solution)/shard_map/ppermute | solution.py:24
  3.6 16.2 %collective-permute-start.1 = (f32[64]{0:T(128)S(1)}, f32[64]{0:T(128)S(1)}, u32[]{:S(2)}, u32[]{:S(2)}) collective-permute-start(f32[64]{0:T(128)S(1)} %get-tuple-element.78), channel_id=1, source_target_pairs={{1,0},{2,1},{3,2},{4,3},{5,4},{6,5},{7,6},{8,7},{9,8},{10,9},{11,1... | collective-permute-start | bytes 776 | tf_op jit(solution)/shard_map/ppermute | solution.py:27
  22.9 1.7 fusion.14
  24.6 7.7 %all-to-all-start = ((f32[8,12,8,128]{3,2,1,0:T(8,128)}), f32[8,12,8,128]{3,2,1,0:T(8,128)}, u32[]{:S(2)}, u32[]{:S(2)}) async-start(f32[8,12,8,128]{3,2,1,0:T(8,128)} %bitcast.120), calls=%async_computation | async-start | bytes 786432 | tf_op jit(solution)/shard_map/all_to_all | solution.py:98
  36.1 2.3 %fusion.7 = f32[16,1,64]{2,1,0:T(1,128)S(1)} fusion(s32[16,64]{1,0:T(8,128)S(1)} %eq.131, s32[16,64]{1,0:T(8,128)S(1)} %eq.127, s32[16,64]{1,0:T(8,128)S(1)} %eq.123, s32[16,64]{1,0:T(8,128)S(1)} %eq.119, s32[16,64]{1,0:T(8,128)S(1)} %eq.115, s32[16,64]{1,0:T(8,128)S(1)} %eq.111, f32[16,192,1]{1,0,2:T(8,128)S(1)} %maximum_bitcast_fusion), kind=kOutput, calls=%fused_computation.17 | convolution fusion | flops 5701632 | bytes 40960 | tf_op jit(solution)/shard_map/bij,bj->bi/dot_general | solution.py:64
  39.8 2.9 %all-to-all-done = f32[8,12,8,128]{3,2,1,0:T(8,128)} async-done(((f32[8,12,8,128]{3,2,1,0:T(8,128)}), f32[8,12,8,128]{3,2,1,0:T(8,128)}, u32[]{:S(2)}, u32[]{:S(2)}) %all-to-all-start) | async-done | bytes 393248 | tf_op jit(solution)/shard_map/all_to_all | solution.py:98
  45.4 1.9 %collective-permute-start.2 = (f32[64]{0:T(128)}, f32[64]{0:T(128)}, u32[]{:S(2)}, u32[]{:S(2)}) collective-permute-start(f32[64]{0:T(128)} %get-tuple-element.73), channel_id=1, source_target_pairs={{0,1},{1,2},{2,3},{3,4},{4,5},{5,6},{6,7},{7,8},{8,9},{9,10},{10,1... | collective-permute-start | bytes 776 | tf_op jit(solution)/shard_map/ppermute | solution.py:24
  47.3 7.0 %collective-permute-start.3 = (f32[64]{0:T(128)}, f32[64]{0:T(128)}, u32[]{:S(2)}, u32[]{:S(2)}) collective-permute-start(f32[64]{0:T(128)} %get-tuple-element.74), channel_id=1, source_target_pairs={{1,0},{2,1},{3,2},{4,3},{5,4},{6,5},{7,6},{8,7},{9,8},{10,9},{11,1... | collective-permute-start | bytes 776 | tf_op jit(solution)/shard_map/ppermute | solution.py:27
  58.9 1.7 fusion.11
  61.6 3.2 %fusion.6 = f32[16,1,64]{2,1,0:T(1,128)S(1)} fusion(s32[16,64]{1,0:T(8,128)} %copy-done.31, s32[16,64]{1,0:T(8,128)} %copy-done.33, s32[16,64]{1,0:T(8,128)} %copy-done.35, s32[16,64]{1,0:T(8,128)} %copy-done.37, s32[16,64]{1,0:T(8,128)} %copy-done.39, s32[16,64]{1,0:T(8,128)} %copy-done.29, f32[16,192,1]{1,0,2:T(8,128)S(1)} %maximum_bitcast_fusion.1), kind=kOutput, calls=%fused_computation.16 | convolution fusion | flops 5701632 | bytes 40960 | tf_op jit(solution)/shard_map/bij,bj->bi/dot_general | solution.py:64
  65.6 1.9 %collective-permute-start.4 = (f32[64]{0:T(128)S(1)}, f32[64]{0:T(128)S(1)}, u32[]{:S(2)}, u32[]{:S(2)}) collective-permute-start(f32[64]{0:T(128)S(1)} %get-tuple-element.69), channel_id=1, source_target_pairs={{0,1},{1,2},{2,3},{3,4},{4,5},{5,6},{6,7},{7,8},{8,9},{9,10},{10,1... | collective-permute-start | bytes 776 | tf_op jit(solution)/shard_map/ppermute | solution.py:24
  67.5 7.0 %collective-permute-start.5 = (f32[64]{0:T(128)S(1)}, f32[64]{0:T(128)S(1)}, u32[]{:S(2)}, u32[]{:S(2)}) collective-permute-start(f32[64]{0:T(128)S(1)} %get-tuple-element.70), channel_id=1, source_target_pairs={{1,0},{2,1},{3,2},{4,3},{5,4},{6,5},{7,6},{8,7},{9,8},{10,9},{11,1... | collective-permute-start | bytes 776 | tf_op jit(solution)/shard_map/ppermute | solution.py:27
  76.7 3.3 %fusion.5 = f32[16,1,64]{2,1,0:T(1,128)S(1)} fusion(s32[16,64]{1,0:T(8,128)} %copy-done.31, s32[16,64]{1,0:T(8,128)} %copy-done.33, s32[16,64]{1,0:T(8,128)} %copy-done.35, s32[16,64]{1,0:T(8,128)} %copy-done.37, s32[16,64]{1,0:T(8,128)} %copy-done.39, s32[16,64]{1,0:T(8,128)} %copy-done.29, f32[16,192,1]{1,0,2:T(8,128)S(1)} %maximum_bitcast_fusion.2), kind=kOutput, calls=%fused_computation.15 | convolution fusion | flops 5701632 | bytes 40960 | tf_op jit(solution)/shard_map/bij,bj->bi/dot_general | solution.py:64
  80.8 1.9 %collective-permute-start.6 = (f32[64]{0:T(128)S(1)}, f32[64]{0:T(128)S(1)}, u32[]{:S(2)}, u32[]{:S(2)}) collective-permute-start(f32[64]{0:T(128)S(1)} %get-tuple-element.65), channel_id=1, source_target_pairs={{0,1},{1,2},{2,3},{3,4},{4,5},{5,6},{6,7},{7,8},{8,9},{9,10},{10,1... | collective-permute-start | bytes 776 | tf_op jit(solution)/shard_map/ppermute | solution.py:24
  82.7 7.0 %collective-permute-start.7 = (f32[64]{0:T(128)S(1)}, f32[64]{0:T(128)S(1)}, u32[]{:S(2)}, u32[]{:S(2)}) collective-permute-start(f32[64]{0:T(128)S(1)} %get-tuple-element.66), channel_id=1, source_target_pairs={{1,0},{2,1},{3,2},{4,3},{5,4},{6,5},{7,6},{8,7},{9,8},{10,9},{11,1... | collective-permute-start | bytes 776 | tf_op jit(solution)/shard_map/ppermute | solution.py:27
  95.1 3.3 %fusion.4 = f32[16,1,64]{2,1,0:T(1,128)S(1)} fusion(s32[16,64]{1,0:T(8,128)} %copy-done.31, s32[16,64]{1,0:T(8,128)} %copy-done.33, s32[16,64]{1,0:T(8,128)} %copy-done.35, s32[16,64]{1,0:T(8,128)} %copy-done.37, s32[16,64]{1,0:T(8,128)} %copy-done.39, s32[16,64]{1,0:T(8,128)} %copy-done.29, f32[16,192,1]{1,0,2:T(8,128)S(1)} %maximum_bitcast_fusion.3), kind=kOutput, calls=%fused_computation.14 | convolution fusion | flops 5701632 | bytes 40960 | tf_op jit(solution)/shard_map/bij,bj->bi/dot_general | solution.py:64
  101.2 1.9 %collective-permute-start.8 = (f32[64]{0:T(128)S(1)}, f32[64]{0:T(128)S(1)}, u32[]{:S(2)}, u32[]{:S(2)}) collective-permute-start(f32[64]{0:T(128)S(1)} %get-tuple-element.61), channel_id=1, source_target_pairs={{0,1},{1,2},{2,3},{3,4},{4,5},{5,6},{6,7},{7,8},{8,9},{9,10},{10,1... | collective-permute-start | bytes 776 | tf_op jit(solution)/shard_map/ppermute | solution.py:24
  103.1 7.0 %collective-permute-start.9 = (f32[64]{0:T(128)S(1)}, f32[64]{0:T(128)S(1)}, u32[]{:S(2)}, u32[]{:S(2)}) collective-permute-start(f32[64]{0:T(128)S(1)} %get-tuple-element.62), channel_id=1, source_target_pairs={{1,0},{2,1},{3,2},{4,3},{5,4},{6,5},{7,6},{8,7},{9,8},{10,9},{11,1... | collective-permute-start | bytes 776 | tf_op jit(solution)/shard_map/ppermute | solution.py:27
  112.3 3.3 %fusion.3 = f32[16,1,64]{2,1,0:T(1,128)S(1)} fusion(s32[16,64]{1,0:T(8,128)} %copy-done.31, s32[16,64]{1,0:T(8,128)} %copy-done.33, s32[16,64]{1,0:T(8,128)} %copy-done.35, s32[16,64]{1,0:T(8,128)} %copy-done.37, s32[16,64]{1,0:T(8,128)} %copy-done.39, s32[16,64]{1,0:T(8,128)} %copy-done.29, f32[16,192,1]{1,0,2:T(8,128)S(1)} %maximum_bitcast_fusion.4), kind=kOutput, calls=%fused_computation.13 | convolution fusion | flops 5701632 | bytes 40960 | tf_op jit(solution)/shard_map/bij,bj->bi/dot_general | solution.py:64
  115.8 1.9 %collective-permute-start.10 = (f32[64]{0:T(128)S(1)}, f32[64]{0:T(128)S(1)}, u32[]{:S(2)}, u32[]{:S(2)}) collective-permute-start(f32[64]{0:T(128)S(1)} %get-tuple-element.57), channel_id=1, source_target_pairs={{0,1},{1,2},{2,3},{3,4},{4,5},{5,6},{6,7},{7,8},{8,9},{9,10},{10,1... | collective-permute-start | bytes 776 | tf_op jit(solution)/shard_map/ppermute | solution.py:24
  117.7 7.0 %collective-permute-start.11 = (f32[64]{0:T(128)S(1)}, f32[64]{0:T(128)S(1)}, u32[]{:S(2)}, u32[]{:S(2)}) collective-permute-start(f32[64]{0:T(128)S(1)} %get-tuple-element.58), channel_id=1, source_target_pairs={{1,0},{2,1},{3,2},{4,3},{5,4},{6,5},{7,6},{8,7},{9,8},{10,9},{11,1... | collective-permute-start | bytes 776 | tf_op jit(solution)/shard_map/ppermute | solution.py:27
  126.3 2.4 %fusion.2 = f32[16,1,64]{2,1,0:T(1,128)S(1)} fusion(s32[16,64]{1,0:T(8,128)S(1)} %copy-done.32, s32[16,64]{1,0:T(8,128)S(1)} %copy-done.34, s32[16,64]{1,0:T(8,128)S(1)} %copy-done.36, s32[16,64]{1,0:T(8,128)S(1)} %copy-done.38, s32[16,64]{1,0:T(8,128)S(1)} %copy-done.40, s32[16,64]{1,0:T(8,128)S(1)} %copy-done.30, f32[16,192,1]{1,0,2:T(8,128)S(1)} %maximum_bitcast_fusion.5), kind=kOutput, calls=%fused_computation.12 | convolution fusion | flops 5701632 | bytes 40960 | tf_op jit(solution)/shard_map/bij,bj->bi/dot_general | solution.py:64
  128.8 1.9 %collective-permute-start.12 = (f32[64]{0:T(128)S(1)}, f32[64]{0:T(128)S(1)}, u32[]{:S(2)}, u32[]{:S(2)}) collective-permute-start(f32[64]{0:T(128)S(1)} %get-tuple-element.53), channel_id=1, source_target_pairs={{0,1},{1,2},{2,3},{3,4},{4,5},{5,6},{6,7},{7,8},{8,9},{9,10},{10,1... | collective-permute-start | bytes 776 | tf_op jit(solution)/shard_map/ppermute | solution.py:24
  130.7 7.0 %collective-permute-start.13 = (f32[64]{0:T(128)S(1)}, f32[64]{0:T(128)S(1)}, u32[]{:S(2)}, u32[]{:S(2)}) collective-permute-start(f32[64]{0:T(128)S(1)} %get-tuple-element.54), channel_id=1, source_target_pairs={{1,0},{2,1},{3,2},{4,3},{5,4},{6,5},{7,6},{8,7},{9,8},{10,9},{11,1... | collective-permute-start | bytes 776 | tf_op jit(solution)/shard_map/ppermute | solution.py:27
  139.3 2.3 %fusion.1 = f32[16,1,64]{2,1,0:T(1,128)S(1)} fusion(s32[16,64]{1,0:T(8,128)S(1)} %copy-done.32, s32[16,64]{1,0:T(8,128)S(1)} %copy-done.34, s32[16,64]{1,0:T(8,128)S(1)} %copy-done.36, s32[16,64]{1,0:T(8,128)S(1)} %copy-done.38, s32[16,64]{1,0:T(8,128)S(1)} %copy-done.40, s32[16,64]{1,0:T(8,128)S(1)} %copy-done.30, f32[16,192,1]{1,0,2:T(8,128)S(1)} %maximum_bitcast_fusion.6), kind=kOutput, calls=%fused_computation.11 | convolution fusion | flops 5701632 | bytes 40960 | tf_op jit(solution)/shard_map/bij,bj->bi/dot_general | solution.py:64
  141.8 1.9 %collective-permute-start.14 = (f32[64]{0:T(128)S(1)}, f32[64]{0:T(128)S(1)}, u32[]{:S(2)}, u32[]{:S(2)}) collective-permute-start(f32[64]{0:T(128)S(1)} %get-tuple-element.49), channel_id=1, source_target_pairs={{0,1},{1,2},{2,3},{3,4},{4,5},{5,6},{6,7},{7,8},{8,9},{9,10},{10,1... | collective-permute-start | bytes 776 | tf_op jit(solution)/shard_map/ppermute | solution.py:24
  143.7 7.0 %collective-permute-start.15 = (f32[64]{0:T(128)S(1)}, f32[64]{0:T(128)S(1)}, u32[]{:S(2)}, u32[]{:S(2)}) collective-permute-start(f32[64]{0:T(128)S(1)} %get-tuple-element.50), channel_id=1, source_target_pairs={{1,0},{2,1},{3,2},{4,3},{5,4},{6,5},{7,6},{8,7},{9,8},{10,9},{11,1... | collective-permute-start | bytes 776 | tf_op jit(solution)/shard_map/ppermute | solution.py:27
  152.2 2.3 %fusion = f32[16,1,64]{2,1,0:T(1,128)S(1)} fusion(s32[16,64]{1,0:T(8,128)S(1)} %copy-done.32, s32[16,64]{1,0:T(8,128)S(1)} %copy-done.34, s32[16,64]{1,0:T(8,128)S(1)} %copy-done.36, s32[16,64]{1,0:T(8,128)S(1)} %copy-done.38, s32[16,64]{1,0:T(8,128)S(1)} %copy-done.40, s32[16,64]{1,0:T(8,128)S(1)} %copy-done.30, f32[16,192,1]{1,0,2:T(8,128)S(1)} %maximum_bitcast_fusion.7), kind=kOutput, calls=%fused_computation.10 | convolution fusion | flops 5701632 | bytes 40960 | tf_op jit(solution)/shard_map/bij,bj->bi/dot_general | solution.py:64
  155.9 5.0 %gather_fusion.1 = f32[1024,3]{1,0:T(8,128)} fusion(f32[3,1024]{0,1:T(8,128)} %copy.54, s32[1024]{0:T(1024)S(1)} %copy-done.26), kind=kCustom, calls=%fused_computation.1 | custom fusion | bytes 28672 | tf_op jit(solution)/shard_map/gather | solution.py:116
  160.9 1.8 %copy.55 = f32[3,8,128]{2,0,1:T(4,128)} copy(f32[3,8,128]{0,2,1:T(8,128)} %bitcast.121) | data formatting | bytes 24576 | tf_op jit(solution)/shard_map/reshape | solution.py:116
  162.7 4.7 %all-to-all-start.1 = ((f32[3,8,128]{2,0,1:T(4,128)}), f32[3,8,128]{2,0,1:T(4,128)S(1)}, u32[]{:S(2)}, u32[]{:S(2)}) async-start(f32[3,8,128]{2,0,1:T(4,128)} %copy.55), calls=%async_computation.1 | async-start | bytes 32768 | tf_op jit(solution)/shard_map/all_to_all | solution.py:117
  168.1 5.7 %all-to-all-done.1 = f32[3,8,128]{2,0,1:T(4,128)S(1)} async-done(((f32[3,8,128]{2,0,1:T(4,128)}), f32[3,8,128]{2,0,1:T(4,128)S(1)}, u32[]{:S(2)}, u32[]{:S(2)}) %all-to-all-start.1) | async-done | bytes 12320 | tf_op jit(solution)/shard_map/all_to_all | solution.py:117
  (224 shorter events, 39.0 us)
Async XLA Ops:
  0.6 22.2 %copy-start = (bf16[1,1,8,12,128,128]{5,4,3,2,1,0:T(8,128)(2,1)S(1)}, bf16[1,1,8,12,128,128]{5,4,3,2,1,0:T(8,128)(2,1)}, u32[]{:S(2)}) copy-start(bf16[1,1,8,12,128,128]{5,4,3,2,1,0:T(8,128)(2,1)} %param.13) | copy-start | bytes 9437188
  0.6 33.9 %copy-start.8 = (f32[1,1,1024]{2,1,0:T(1,128)S(1)}, f32[1,1,1024]{2,1,0:T(1,128)}, u32[]{:S(2)}) copy-start(f32[1,1,1024]{2,1,0:T(1,128)} %param.19) | copy-start | bytes 12292
  0.7 32.1 %copy-start.42 = (s32[1,1,1024]{2,1,0:T(1,128)S(1)}, s32[1,1,1024]{2,1,0:T(1,128)}, u32[]{:S(2)}) copy-start(s32[1,1,1024]{2,1,0:T(1,128)} %param.21) | copy-start | bytes 12292
  0.7 32.7 %copy-start.25 = (s32[1,1,6,1024]{3,1,2,0:T(1,128)S(1)}, s32[1,1,6,1024]{3,1,2,0:T(1,128)}, u32[]{:S(2)}) copy-start(s32[1,1,6,1024]{3,1,2,0:T(1,128)} %param.20) | copy-start | bytes 73732
  0.7 33.3 %copy-start.41 = (s32[1,1,8,12]{3,2,1,0:T(8,128)S(1)}, s32[1,1,8,12]{3,2,1,0:T(8,128)}, u32[]{:S(2)}) copy-start(s32[1,1,8,12]{3,2,1,0:T(8,128)} %param.15) | copy-start | bytes 1156
  1.6 34.2 %collective-permute-start = (f32[64]{0:T(128)S(1)}, f32[64]{0:T(128)S(1)}, u32[]{:S(2)}, u32[]{:S(2)}) collective-permute-start(f32[64]{0:T(128)S(1)} %get-tuple-element.77), channel_id=1, source_target_pairs={{0,1},{1,2},{2,3},{3,4},{4,5},{5,6},{6,7},{7,8},{8,9},{9,10},{10,1... | collective-permute-start | bytes 776 | tf_op jit(solution)/shard_map/ppermute | solution.py:24
  3.6 32.1 %collective-permute-start.1 = (f32[64]{0:T(128)S(1)}, f32[64]{0:T(128)S(1)}, u32[]{:S(2)}, u32[]{:S(2)}) collective-permute-start(f32[64]{0:T(128)S(1)} %get-tuple-element.78), channel_id=1, source_target_pairs={{1,0},{2,1},{3,2},{4,3},{5,4},{6,5},{7,6},{8,7},{9,8},{10,9},{11,1... | collective-permute-start | bytes 776 | tf_op jit(solution)/shard_map/ppermute | solution.py:27
  24.6 32.9 %copy-start.1 = (f32[1,1,47,1024]{3,1,2,0:T(1,128)S(1)}, f32[1,1,47,1024]{3,1,2,0:T(1,128)}, u32[]{:S(2)}) copy-start(f32[1,1,47,1024]{3,1,2,0:T(1,128)} %param.18) | copy-start | bytes 577540
  24.6 18.2 %all-to-all-start = ((f32[8,12,8,128]{3,2,1,0:T(8,128)}), f32[8,12,8,128]{3,2,1,0:T(8,128)}, u32[]{:S(2)}, u32[]{:S(2)}) async-start(f32[8,12,8,128]{3,2,1,0:T(8,128)} %bitcast.120), calls=%async_computation | async-start | bytes 786432 | tf_op jit(solution)/shard_map/all_to_all | solution.py:98
  35.4 18.9 %copy-start.29 = (s32[16,64]{1,0:T(8,128)}, s32[16,64]{1,0:T(8,128)S(1)}, u32[]{:S(2)}) copy-start(s32[16,64]{1,0:T(8,128)S(1)} %eq.111) | copy-start | bytes 12292
  35.5 18.8 %copy-start.31 = (s32[16,64]{1,0:T(8,128)}, s32[16,64]{1,0:T(8,128)S(1)}, u32[]{:S(2)}) copy-start(s32[16,64]{1,0:T(8,128)S(1)} %eq.131) | copy-start | bytes 12292
  35.5 18.7 %copy-start.33 = (s32[16,64]{1,0:T(8,128)}, s32[16,64]{1,0:T(8,128)S(1)}, u32[]{:S(2)}) copy-start(s32[16,64]{1,0:T(8,128)S(1)} %eq.127) | copy-start | bytes 12292
  35.6 18.7 %copy-start.35 = (s32[16,64]{1,0:T(8,128)}, s32[16,64]{1,0:T(8,128)S(1)}, u32[]{:S(2)}) copy-start(s32[16,64]{1,0:T(8,128)S(1)} %eq.123) | copy-start | bytes 12292
  35.7 18.6 %copy-start.37 = (s32[16,64]{1,0:T(8,128)}, s32[16,64]{1,0:T(8,128)S(1)}, u32[]{:S(2)}) copy-start(s32[16,64]{1,0:T(8,128)S(1)} %eq.119) | copy-start | bytes 12292
  35.8 18.6 %copy-start.39 = (s32[16,64]{1,0:T(8,128)}, s32[16,64]{1,0:T(8,128)S(1)}, u32[]{:S(2)}) copy-start(s32[16,64]{1,0:T(8,128)S(1)} %eq.115) | copy-start | bytes 12292
  45.4 15.3 %collective-permute-start.2 = (f32[64]{0:T(128)}, f32[64]{0:T(128)}, u32[]{:S(2)}, u32[]{:S(2)}) collective-permute-start(f32[64]{0:T(128)} %get-tuple-element.73), channel_id=1, source_target_pairs={{0,1},{1,2},{2,3},{3,4},{4,5},{5,6},{6,7},{7,8},{8,9},{9,10},{10,1... | collective-permute-start | bytes 776 | tf_op jit(solution)/shard_map/ppermute | solution.py:24
  47.3 13.4 %collective-permute-start.3 = (f32[64]{0:T(128)}, f32[64]{0:T(128)}, u32[]{:S(2)}, u32[]{:S(2)}) collective-permute-start(f32[64]{0:T(128)} %get-tuple-element.74), channel_id=1, source_target_pairs={{1,0},{2,1},{3,2},{4,3},{5,4},{6,5},{7,6},{8,7},{9,8},{10,9},{11,1... | collective-permute-start | bytes 776 | tf_op jit(solution)/shard_map/ppermute | solution.py:27
  65.6 10.0 %collective-permute-start.4 = (f32[64]{0:T(128)S(1)}, f32[64]{0:T(128)S(1)}, u32[]{:S(2)}, u32[]{:S(2)}) collective-permute-start(f32[64]{0:T(128)S(1)} %get-tuple-element.69), channel_id=1, source_target_pairs={{0,1},{1,2},{2,3},{3,4},{4,5},{5,6},{6,7},{7,8},{8,9},{9,10},{10,1... | collective-permute-start | bytes 776 | tf_op jit(solution)/shard_map/ppermute | solution.py:24
  67.5 8.2 %collective-permute-start.5 = (f32[64]{0:T(128)S(1)}, f32[64]{0:T(128)S(1)}, u32[]{:S(2)}, u32[]{:S(2)}) collective-permute-start(f32[64]{0:T(128)S(1)} %get-tuple-element.70), channel_id=1, source_target_pairs={{1,0},{2,1},{3,2},{4,3},{5,4},{6,5},{7,6},{8,7},{9,8},{10,9},{11,1... | collective-permute-start | bytes 776 | tf_op jit(solution)/shard_map/ppermute | solution.py:27
  80.8 9.9 %collective-permute-start.6 = (f32[64]{0:T(128)S(1)}, f32[64]{0:T(128)S(1)}, u32[]{:S(2)}, u32[]{:S(2)}) collective-permute-start(f32[64]{0:T(128)S(1)} %get-tuple-element.65), channel_id=1, source_target_pairs={{0,1},{1,2},{2,3},{3,4},{4,5},{5,6},{6,7},{7,8},{8,9},{9,10},{10,1... | collective-permute-start | bytes 776 | tf_op jit(solution)/shard_map/ppermute | solution.py:24
  82.7 8.2 %collective-permute-start.7 = (f32[64]{0:T(128)S(1)}, f32[64]{0:T(128)S(1)}, u32[]{:S(2)}, u32[]{:S(2)}) collective-permute-start(f32[64]{0:T(128)S(1)} %get-tuple-element.66), channel_id=1, source_target_pairs={{1,0},{2,1},{3,2},{4,3},{5,4},{6,5},{7,6},{8,7},{9,8},{10,9},{11,1... | collective-permute-start | bytes 776 | tf_op jit(solution)/shard_map/ppermute | solution.py:27
  101.2 9.7 %collective-permute-start.8 = (f32[64]{0:T(128)S(1)}, f32[64]{0:T(128)S(1)}, u32[]{:S(2)}, u32[]{:S(2)}) collective-permute-start(f32[64]{0:T(128)S(1)} %get-tuple-element.61), channel_id=1, source_target_pairs={{0,1},{1,2},{2,3},{3,4},{4,5},{5,6},{6,7},{7,8},{8,9},{9,10},{10,1... | collective-permute-start | bytes 776 | tf_op jit(solution)/shard_map/ppermute | solution.py:24
  103.1 8.2 %collective-permute-start.9 = (f32[64]{0:T(128)S(1)}, f32[64]{0:T(128)S(1)}, u32[]{:S(2)}, u32[]{:S(2)}) collective-permute-start(f32[64]{0:T(128)S(1)} %get-tuple-element.62), channel_id=1, source_target_pairs={{1,0},{2,1},{3,2},{4,3},{5,4},{6,5},{7,6},{8,7},{9,8},{10,9},{11,1... | collective-permute-start | bytes 776 | tf_op jit(solution)/shard_map/ppermute | solution.py:27
  112.3 25.4 %copy-start.7 = (f32[16,64]{1,0:T(8,128)S(1)}, f32[16,64]{1,0:T(8,128)}, u32[]{:S(2)}) copy-start(f32[16,64]{1,0:T(8,128)} %get-tuple-element.42) | copy-start | bytes 12292
  115.8 9.2 %collective-permute-start.10 = (f32[64]{0:T(128)S(1)}, f32[64]{0:T(128)S(1)}, u32[]{:S(2)}, u32[]{:S(2)}) collective-permute-start(f32[64]{0:T(128)S(1)} %get-tuple-element.57), channel_id=1, source_target_pairs={{0,1},{1,2},{2,3},{3,4},{4,5},{5,6},{6,7},{7,8},{8,9},{9,10},{10,1... | collective-permute-start | bytes 776 | tf_op jit(solution)/shard_map/ppermute | solution.py:24
  117.7 8.2 %collective-permute-start.11 = (f32[64]{0:T(128)S(1)}, f32[64]{0:T(128)S(1)}, u32[]{:S(2)}, u32[]{:S(2)}) collective-permute-start(f32[64]{0:T(128)S(1)} %get-tuple-element.58), channel_id=1, source_target_pairs={{1,0},{2,1},{3,2},{4,3},{5,4},{6,5},{7,6},{8,7},{9,8},{10,9},{11,1... | collective-permute-start | bytes 776 | tf_op jit(solution)/shard_map/ppermute | solution.py:27
  128.8 9.2 %collective-permute-start.12 = (f32[64]{0:T(128)S(1)}, f32[64]{0:T(128)S(1)}, u32[]{:S(2)}, u32[]{:S(2)}) collective-permute-start(f32[64]{0:T(128)S(1)} %get-tuple-element.53), channel_id=1, source_target_pairs={{0,1},{1,2},{2,3},{3,4},{4,5},{5,6},{6,7},{7,8},{8,9},{9,10},{10,1... | collective-permute-start | bytes 776 | tf_op jit(solution)/shard_map/ppermute | solution.py:24
  130.7 8.2 %collective-permute-start.13 = (f32[64]{0:T(128)S(1)}, f32[64]{0:T(128)S(1)}, u32[]{:S(2)}, u32[]{:S(2)}) collective-permute-start(f32[64]{0:T(128)S(1)} %get-tuple-element.54), channel_id=1, source_target_pairs={{1,0},{2,1},{3,2},{4,3},{5,4},{6,5},{7,6},{8,7},{9,8},{10,9},{11,1... | collective-permute-start | bytes 776 | tf_op jit(solution)/shard_map/ppermute | solution.py:27
  141.6 25.8 %copy-start.27 = (f32[1,1,1024]{2,1,0:T(1,128)S(1)}, f32[1,1,1024]{2,1,0:T(1,128)}, u32[]{:S(2)}) copy-start(f32[1,1,1024]{2,1,0:T(1,128)} %div.107) | copy-start | bytes 12292
  141.8 9.2 %collective-permute-start.14 = (f32[64]{0:T(128)S(1)}, f32[64]{0:T(128)S(1)}, u32[]{:S(2)}, u32[]{:S(2)}) collective-permute-start(f32[64]{0:T(128)S(1)} %get-tuple-element.49), channel_id=1, source_target_pairs={{0,1},{1,2},{2,3},{3,4},{4,5},{5,6},{6,7},{7,8},{8,9},{9,10},{10,1... | collective-permute-start | bytes 776 | tf_op jit(solution)/shard_map/ppermute | solution.py:24
  143.7 8.2 %collective-permute-start.15 = (f32[64]{0:T(128)S(1)}, f32[64]{0:T(128)S(1)}, u32[]{:S(2)}, u32[]{:S(2)}) collective-permute-start(f32[64]{0:T(128)S(1)} %get-tuple-element.50), channel_id=1, source_target_pairs={{1,0},{2,1},{3,2},{4,3},{5,4},{6,5},{7,6},{8,7},{9,8},{10,9},{11,1... | collective-permute-start | bytes 776 | tf_op jit(solution)/shard_map/ppermute | solution.py:27
  162.7 11.1 %all-to-all-start.1 = ((f32[3,8,128]{2,0,1:T(4,128)}), f32[3,8,128]{2,0,1:T(4,128)S(1)}, u32[]{:S(2)}, u32[]{:S(2)}) async-start(f32[3,8,128]{2,0,1:T(4,128)} %copy.55), calls=%async_computation.1 | async-start | bytes 32768 | tf_op jit(solution)/shard_map/all_to_all | solution.py:117
  (29 other events, 249.4 us)
where the time goes:
time: 176 us; the launch traced here: 174 us
  starting transfers between devices  92.7 us (53%)
  matrix products  25.3 us (14%)
  local copies, waits for them, and re-layouts  24 us (14%)
  other arithmetic  18.5 us (11%)
  waiting for transfers between devices  12.4 us (7%)
    ppermute x8, starting transfers between devices, extended_2(): lax.ppermute(lax.slice_in_dim(block, 0, width, axis=dim), axis, backward)  65 us
    dot_general x8, matrix products, neighbour_mean(): jnp.einsum('bij,bj->bi', tiles, windows, precision=lax.Precision.HIGHEST)  22.4 us
    ppermute x8, starting transfers between devices, extended_2(): lax.ppermute(lax.slice_in_dim(block, block.shape[dim] - width, None, axis...  15.4 us
    all_to_all x1, starting transfers between devices, per_device(): lax.all_to_all(terms, 'comp', split_axis=0, concat_axis=0, tiled=True)  7.68 us
    all_to_all x1, waiting for transfers between devices, per_device(): lax.all_to_all(permuted, 'comp', split_axis=1, concat_axis=1, tiled=True)  5.74 us
    gather x1, local copies, waits for them, and re-layouts, per_device(): permuted = state[:, coupler_perm[0, 0]].reshape(3, groups, cells // groups)  5.03 us
    all_to_all x1, starting transfers between devices, per_device(): lax.all_to_all(permuted, 'comp', split_axis=1, concat_axis=1, tiled=True)  4.69 us
    div x23, local copies, waits for them, and re-layouts, neighbour_mean(): return summed.reshape(-1) / 6.0  4.19 us
  transfers between devices with their start and end apart: 18, of which 8 were waited for; matrix products, arithmetic and copies ran while one was open for 13% of the time, Pallas kernels for 0%

commit v1 on v0

v1 whole, which is shorter than its diff:
```python
import jax
import jax.numpy as jnp
from jax import lax
from jax.experimental import pallas as pl
from jax.experimental.pallas import tpu as pltpu
from jax.sharding import PartitionSpec as P

SUB = 8
MIX = 4
LANES = 128
FIELDS = 5

heat_gain = 0.5
shortwave_gain = 0.5
wind_mixing = 0.15
relax_rate = 0.5
fresh_gain = 0.5


def shape_of(dims, dtype=jnp.float32):
    return jax.ShapeDtypeStruct(dims, dtype)


def terms_kernel(src_ref, cnt_ref, flux_ref, weight_ref, out_ref, blocks_ref, term_ref):
    d = pl.program_id(0)
    slots = weight_ref.shape[1]
    nb = blocks_ref.shape[0]

    @pl.when(d == 0)
    def _():
        for b in range(nb):
            blocks_ref[b] = flux_ref[:, b * LANES : (b + 1) * LANES].astype(jnp.float32)

    lane = lax.broadcasted_iota(jnp.int32, (8, LANES), 1)
    zero = jnp.zeros((8, LANES), jnp.float32)
    for k in range(0, slots, 2):
        parts = []
        for i in (0, 1):
            block = blocks_ref[src_ref[0, 0, d, k + i]]
            parts.append(jnp.where(lane < cnt_ref[0, 0, d, k + i], block, zero))
        top = jnp.concatenate([parts[0], zero], axis=1)
        low = jnp.concatenate([zero, parts[1]], axis=1)
        lhs = jnp.concatenate([top, low], axis=0).astype(jnp.bfloat16)
        rhs = weight_ref[0, k : k + 2].reshape(2 * LANES, LANES)
        term_ref[k * 8 : k * 8 + 16, :] = jnp.dot(lhs, rhs, preferred_element_type=jnp.float32)

    def field(f):
        return term_ref[pl.ds(f, slots, stride=8), :]

    out_ref[0, 0:slots] = field(1)
    out_ref[0, slots : 2 * slots] = field(0) + field(7)
    out_ref[0, 2 * slots : 3 * slots] = field(2)
    out_ref[0, 3 * slots : 4 * slots] = field(3)
    out_ref[0, 4 * slots : 5 * slots] = field(5) - field(4) + field(6)
    rest = out_ref.shape[1] - FIELDS * slots
    if rest:
        out_ref[0, FIELDS * slots :] = jnp.zeros((rest, LANES), jnp.float32)


def remap_terms(src, cnt, flux, weights):
    groups, slots = weights.shape[:2]
    rows = -(-FIELDS * slots // 8) * 8
    smem = pl.BlockSpec(memory_space=pltpu.SMEM)
    return pl.pallas_call(
        terms_kernel,
        grid=(groups,),
        in_specs=[
            smem,
            smem,
            pl.BlockSpec(flux.shape, lambda d: (0, 0)),
            pl.BlockSpec((1,) + weights.shape[1:], lambda d: (d, 0, 0, 0)),
        ],
        out_specs=pl.BlockSpec((1, rows, LANES), lambda d: (d, 0, 0)),
        out_shape=shape_of((groups, rows, LANES)),
        scratch_shapes=[
            pltpu.VMEM((flux.shape[1] // LANES, 8, LANES), jnp.float32),
            pltpu.VMEM((slots * 8, LANES), jnp.float32),
        ],
    )(src, cnt, flux, weights)


def forcing_kernel(odd_ref, arrived_ref, dst_ref, ssh_ref, off_ref, forcing_ref, offs_ref, pay0_ref, pay1_ref):
    groups, rows, _ = arrived_ref.shape
    slots = dst_ref.shape[1]
    dst = dst_ref[...]
    parts = [dst + 8 * f for f in range(FIELDS)]
    rest = rows - FIELDS * slots
    if rest:
        parts.append(jnp.full((groups, rest), -1, jnp.int32))
    ids = jnp.concatenate(parts, axis=1)
    targets = lax.broadcasted_iota(jnp.int32, (FIELDS * 8, rows), 0)
    total = jnp.zeros((FIELDS * 8, LANES), jnp.float32)
    for c in range(groups):
        onehot = (jnp.broadcast_to(ids[c : c + 1, :], targets.shape) == targets).astype(jnp.float32)
        onehot = onehot.astype(jnp.bfloat16)
        rest_of = arrived_ref[c]
        for _ in range(3):
            piece = rest_of.astype(jnp.bfloat16)
            total = total + jnp.dot(onehot, piece, preferred_element_type=jnp.float32)
            rest_of = rest_of - piece.astype(jnp.float32)
    forcing_ref[...] = total
    offsets = off_ref.shape[0]
    for b in range(8):
        cols = off_ref[:, b * LANES : (b + 1) * LANES].astype(jnp.float32)
        offs_ref[pl.ds(b, offsets, stride=8), :] = cols
    odd = odd_ref[0] == 1
    pieces = [ssh_ref[...], total[(FIELDS - 1) * 8 :]]
    pieces += [offs_ref[j * 8 : j * 8 + 8, :] for j in range(offsets)]
    for i, x in enumerate(pieces):
        pay0_ref[4 * i : 4 * i + 4, :] = jnp.where(odd, x[0:4], x[4:8])
        pay1_ref[4 * i : 4 * i + 4, :] = jnp.where(odd, x[4:8], x[0:4])


def forcing_and_halo(odd, arrived, dst, ssh, offsets):
    vmem = pl.BlockSpec(memory_space=pltpu.VMEM)
    count = offsets.shape[0]
    pay = shape_of((4 * (2 + count), LANES))
    return pl.pallas_call(
        forcing_kernel,
        in_specs=[pl.BlockSpec(memory_space=pltpu.SMEM)] + [vmem] * 4,
        out_specs=[vmem] * 4,
        out_shape=[shape_of((FIELDS * 8, LANES)), shape_of((count * 8, LANES)), pay, pay],
    )(odd, arrived, dst, ssh, offsets)


def column_kernel(temp_ref, kappa_ref, forcing_ref, mixed_ref, top_ref):
    levels = temp_ref.shape[0]
    level = lax.broadcasted_iota(jnp.int32, (levels, LANES), 0)
    depth = level.astype(jnp.float32)
    decay = jnp.exp(-depth / 4.0)
    shallow = shortwave_gain * (decay - jnp.exp(-(depth + 1.0) / 4.0))
    decay = jnp.where(level < levels - 1, decay, 0.0)
    east, north = forcing_ref[16:24, :], forcing_ref[24:32, :]
    mixing = wind_mixing * jnp.tanh(jnp.sqrt(east * east + north * north))
    top = heat_gain * forcing_ref[8:16, :]
    short = forcing_ref[0:8, :]
    last = jnp.zeros((1, LANES), jnp.float32)
    for b in range(temp_ref.shape[1] // LANES):
        cols = slice(b * LANES, (b + 1) * LANES)

        def row(x):
            return jnp.broadcast_to(x[b : b + 1, :], (levels, LANES))

        heated = temp_ref[:, cols] + row(short) * shallow
        heated = heated + jnp.where(level == 0, row(top), 0.0)
        keff = jnp.concatenate([kappa_ref[:, cols], last], axis=0) + row(mixing) * decay
        for _ in range(MIX):
            flow = keff * (pltpu.roll(heated, levels - 1, 0) - heated)
            heated = heated + flow - pltpu.roll(flow, 1, 0)
        mixed_ref[:, cols] = heated
        top_ref[b : b + 1, :] = heated[0:1]
        top_ref[8 + b : 9 + b, :] = heated[1:2]


def column_update(temp, kappa, forcing):
    vmem = pl.BlockSpec(memory_space=pltpu.VMEM)
    return pl.pallas_call(
        column_kernel,
        in_specs=[vmem] * 3,
        out_specs=[vmem] * 2,
        out_shape=[shape_of(temp.shape), shape_of((16, LANES))],
        cost_estimate=pl.CostEstimate(
            flops=40 * temp.size, bytes_accessed=12 * temp.size, transcendentals=2048
        ),
    )(temp, kappa, forcing)


def pick(x, idx):
    return jnp.take_along_axis(x, idx, axis=1, mode="promise_in_bounds")


def height_kernel(odd_ref, got0_ref, got1_ref, ssh_ref, fresh_ref, offs_ref, top_ref, perm_ref, ssh_out, state_out):
    odd = odd_ref[0] == 1
    count = offs_ref.shape[0] // 8

    def extended(i, own):
        a, b = got0_ref[4 * i : 4 * i + 4, :], got1_ref[4 * i : 4 * i + 4, :]
        left, right = jnp.where(odd, a, b), jnp.where(odd, b, a)
        return jnp.concatenate([left, own, right], axis=0)

    eta = extended(0, ssh_ref[...])
    fresh = (fresh_gain / SUB) * extended(1, fresh_ref[...])
    lane = lax.broadcasted_iota(jnp.int32, (16, LANES), 1)
    places, crossing = [], []
    for j in range(count):
        target = lane + extended(2 + j, offs_ref[j * 8 : j * 8 + 8, :]).astype(jnp.int32)
        places.append(target & (LANES - 1))
        crossing.append((target < 0) | (target >= LANES))
    upper = lane >= LANES // 2
    for _ in range(SUB):
        beside = jnp.where(upper, pltpu.roll(eta, 1, 0), pltpu.roll(eta, 15, 0))
        halves = []
        for h in (0, 8):
            here, other = eta[h : h + 8], beside[h : h + 8]
            near = None
            for j in range(count):
                idx = places[j][h : h + 8]
                value = jnp.where(crossing[j][h : h + 8], pick(other, idx), pick(here, idx))
                near = value if near is None else near + value
            halves.append(near)
        average = jnp.concatenate(halves, axis=0) / 6.0
        eta = eta + relax_rate * (average - eta) + fresh
    height = eta[4:12]
    ssh_out[...] = height
    perm = perm_ref[...]
    row, col = perm >> 7, perm & (LANES - 1)
    for f, x in enumerate((top_ref[0:8, :], top_ref[8:16, :], height)):
        out = jnp.zeros((8, LANES), jnp.float32)
        for s in range(8):
            out = jnp.where(row == s, pick(jnp.broadcast_to(x[s : s + 1, :], (8, LANES)), col), out)
        for d in range(8):
            state_out[d, f : f + 1, :] = out[d : d + 1]


def heights_and_state(odd, got0, got1, ssh, fresh, offs, top, perm):
    vmem = pl.BlockSpec(memory_space=pltpu.VMEM)
    return pl.pallas_call(
        height_kernel,
        in_specs=[pl.BlockSpec(memory_space=pltpu.SMEM)] + [vmem] * 7,
        out_specs=[vmem] * 2,
        out_shape=[shape_of((8, LANES)), shape_of((8, 3, LANES))],
    )(odd, got0, got1, ssh, fresh, offs, top, perm)


def per_device(
    atm_flux,
    intersection_weight,
    src_block,
    dst_block,
    intersection_count,
    temp,
    kappa,
    ssh,
    nbr_offset,
    coupler_perm,
):
    tiles = lax.axis_size("tile")
    odd = (lax.axis_index("tile") % 2).astype(jnp.int32).reshape(1)
    height = ssh.reshape(8, LANES)
    perm = coupler_perm.reshape(8, LANES)
    terms = remap_terms(src_block, intersection_count, atm_flux[0, 0], intersection_weight[0, 0])
    arrived = lax.all_to_all(terms, "comp", split_axis=0, concat_axis=0, tiled=True)
    forcing, offs, pay0, pay1 = forcing_and_halo(
        odd, arrived, dst_block[0, 0], height, nbr_offset[0, 0]
    )
    inner = [(i, i ^ 1) for i in range(tiles)]
    outer = [(i, (i - 1 if i % 2 == 0 else i + 1) % tiles) for i in range(tiles)]
    got1 = lax.ppermute(pay1, "tile", outer)
    got0 = lax.ppermute(pay0, "tile", inner)
    mixed, top = column_update(temp[0, 0], kappa[0, 0], forcing)
    height, state = heights_and_state(
        odd, got0, got1, height, forcing[(FIELDS - 1) * 8 :], offs, top, perm
    )
    relaid = lax.all_to_all(state, "comp", split_axis=0, concat_axis=0, tiled=True)
    coupler_state = relaid.transpose(1, 0, 2).reshape(1, 1, 3, -1)
    return (mixed[None, None], height.reshape(ssh.shape), coupler_state)


def solution(mesh):
    return jax.shard_map(
        per_device,
        mesh=mesh,
        in_specs=(
            P("comp", "tile", None, None),
            P("comp", "tile", None, None, None, None),
            P("comp", "tile", None, None),
            P("comp", "tile", None, None),
            P("comp", "tile", None, None),
            P("comp", "tile", None, None),
            P("comp", "tile", None, None),
            P("comp", "tile", None),
            P("comp", "tile", None, None),
            P("comp", "tile", None),
        ),
        out_specs=(
            P("comp", "tile", None, None),
            P("comp", "tile", None),
            P("comp", "tile", None, None),
        ),
        check_vma=False,
    )
```

time: 176 us -> 65.5 us (0.37)
  starting transfers between devices: 92.7 us -> 27.7 us
  matrix products: 25.3 us -> 0 us
  local copies, waits for them, and re-layouts: 24 us -> 4.52 us
  other arithmetic: 18.5 us -> 0 us
  Pallas kernels: 0 us -> 12.5 us
  blocking collectives: 0 us -> 11 us
  waiting for transfers between devices: 12.4 us -> 8.43 us
    ppermute x16 -> x2, starting transfers between devices: 80.4 us -> 14.9 us  [the longest x1 13 us: per_device(): got1 = lax.ppermute(pay1, 'tile', outer)]
    dot_general x10 -> x0, matrix products: 25.3 us -> none  [the longest x8 22.4 us: neighbour_mean(): jnp.einsum('bij,bj->bi', tiles, windows, precision=lax.Precision.HIGHEST)]
    pallas_call x0 -> x4, Pallas kernels: none -> 12.5 us  [the longest x1 6.14 us: remap_terms(): pl.pallas_call(terms_kernel, grid=(groups,), in_specs=[smem, smem, pl.Blo...]
    all_to_all x0 -> x1, blocking collectives: none -> 11 us  [per_device(): lax.all_to_all(state, 'comp', split_axis=0, concat_axis=0, tiled=True)]
    gather x2 -> x0, local copies, waits for them, and re-layouts: 6.41 us -> none  [the longest x1 5.03 us: per_device(): permuted = state[:, coupler_perm[0, 0]].reshape(3, groups, cells // groups)]
    all_to_all x1 -> x0, waiting for transfers between devices: 5.74 us -> none  [per_device(): lax.all_to_all(permuted, 'comp', split_axis=1, concat_axis=1, tiled=True)]
    add x20 -> x0, other arithmetic: 5.62 us -> none  [the longest x16 3.3 us: per_device(): height = height + relax_rate * (average - height) + fresh_gain * fresh / SUB]
    all_to_all x1, waiting for transfers between devices: 2.93 us -> 8.43 us  [per_device(): lax.all_to_all(terms, 'comp', split_axis=0, concat_axis=0, tiled=True)]
  transfers between devices with their start and end apart: 18 -> 3, of which waited for: 8 -> 1; matrix products, arithmetic and copies ran while one was open for 13% -> 4% of each run, Pallas kernels for 0% -> 3%
where the time goes in v1:
time: 65.5 us; the launch traced here: 64.9 us
  starting transfers between devices  27.7 us (42%)
  Pallas kernels  12.5 us (19%)
  blocking collectives  11 us (17%)
  waiting for transfers between devices  8.43 us (13%)
  local copies, waits for them, and re-layouts  4.52 us (7%)
  between operations  0.69 us (1%)
    ppermute x1, starting transfers between devices, per_device(): got1 = lax.ppermute(pay1, 'tile', outer)  13 us
    all_to_all x1, starting transfers between devices, per_device(): lax.all_to_all(terms, 'comp', split_axis=0, concat_axis=0, tiled=True)  12.8 us
    all_to_all x1, blocking collectives, per_device(): lax.all_to_all(state, 'comp', split_axis=0, concat_axis=0, tiled=True)  11 us
    all_to_all x1, waiting for transfers between devices, per_device(): lax.all_to_all(terms, 'comp', split_axis=0, concat_axis=0, tiled=True)  8.43 us
    pallas_call x1, Pallas kernels, remap_terms(): pl.pallas_call(terms_kernel, grid=(groups,), in_specs=[smem, smem, pl.Blo...  6.14 us
    unnamed x13, local copies, waits for them, and re-layouts  3.26 us
    pallas_call x1, Pallas kernels, heights_and_state(): pl.pallas_call(height_kernel, in_specs=[pl.BlockSpec(memory_space=pltpu.S...  2.49 us
    pallas_call x1, Pallas kernels, column_update(): pl.pallas_call(column_kernel, in_specs=[vmem] * 3, out_specs=[vmem] * 2,...  1.96 us
  transfers between devices with their start and end apart: 3, of which 1 were waited for; matrix products, arithmetic and copies ran while one was open for 4% of the time, Pallas kernels for 3%

profile of v1, /device:TPU:8, one launch (start us, length us, event | category | flops | bytes accessed | tf_op | source)
XLA Modules:
  0.0 64.9 jit_solution(2393953215551120350)
XLA Ops:
  0.6 0.0 copy-start.2
  0.6 0.0 copy-start.1
  0.7 6.1 %shard_map.121 = f32[8,64,128]{2,1,0:T(8,128)} custom-call(s32[1,1,8,12]{3,2,1,0:T(8,128)} %src_ref.1, s32[1,1,8,12]{3,2,1,0:T(8,128)} %cnt_ref.1, bf16[8,1024]{1,0:T(8,128)(2,1)} %bitcast.23, bf16[8,12,128,128]{3,2,1,0:T(8,128)(2,1)} %bitcast.18), custom_call_target="tpu_custom_call" | custom-call | tf_op jit(solution)/shard_map/pallas_call | solution.py:64
  6.8 12.8 %all-to-all-start = ((f32[8,64,128]{2,1,0:T(8,128)}), f32[8,64,128]{2,1,0:T(8,128)S(1)}, u32[]{:S(2)}, u32[]{:S(2)}) async-start(f32[8,64,128]{2,1,0:T(8,128)} %shard_map.121), calls=%async_computation | async-start | bytes 524288 | tf_op jit(solution)/shard_map/all_to_all | solution.py:242
  19.6 0.0 copy-done.2
  19.6 0.6 copy.19
  20.2 8.4 %all-to-all-done.arrived_ref = f32[8,64,128]{2,1,0:T(8,128)S(1)} async-done(((f32[8,64,128]{2,1,0:T(8,128)}), f32[8,64,128]{2,1,0:T(8,128)S(1)}, u32[]{:S(2)}, u32[]{:S(2)}) %all-to-all-start) | async-done | bytes 262176 | tf_op jit(solution)/shard_map/all_to_all | solution.py:242
  28.6 0.0 copy-start
  28.6 0.7 %copy-done = f32[8,64,128]{2,1,0:T(8,128)} copy-done((f32[8,64,128]{2,1,0:T(8,128)}, f32[8,64,128]{2,1,0:T(8,128)S(1)}, u32[]{:S(2)}) %copy-start) | copy-done | bytes 262168
  29.3 2.0 %shard_map.122 = (f32[40,128]{1,0:T(8,128)}, f32[48,128]{1,0:T(8,128)}, f32[32,128]{1,0:T(8,128)}, f32[32,128]{1,0:T(8,128)}) custom-call(s32[1]{0:T(128)} %bitcast.1.odd_ref, f32[8,64,128]{2,1,0:T(8,128)} %copy-done, s32[8,12]{1,0:T(8,128)} %bitcast.26, f32[8,128]{1,0:T(8,128)} %bitcast.24, s32[6,1024]{1,0:T(8,128)} %bitcast.21), custom_call_target="tpu_custom_call" | custom-call | tf_op jit(solution)/shard_map/pallas_call | solution.py:118
  31.3 1.9 %collective-permute-start = (f32[32,128]{1,0:T(8,128)}, f32[32,128]{1,0:T(8,128)S(1)}, u32[]{:S(2)}, u32[]{:S(2)}) collective-permute-start(f32[32,128]{1,0:T(8,128)} %get-tuple-element.13), channel_id=1, source_target_pairs={{0,1},{1,0},{2,3},{3,2},{4,5},{5,4},{6,7},{7,6},{8,9},{9,8},{10,11... | collective-permute-start | bytes 49160 | tf_op jit(solution)/shard_map/ppermute | solution.py:249
  33.2 13.0 %collective-permute-start.1 = (f32[32,128]{1,0:T(8,128)}, f32[32,128]{1,0:T(8,128)S(1)}, u32[]{:S(2)}, u32[]{:S(2)}) collective-permute-start(f32[32,128]{1,0:T(8,128)} %get-tuple-element.14), channel_id=1, source_target_pairs={{0,95},{1,2},{2,1},{3,4},{4,3},{5,6},{6,5},{7,8},{8,7},{9,10},{10,... | collective-permute-start | bytes 49160 | tf_op jit(solution)/shard_map/ppermute | solution.py:248
  46.2 0.0 copy-done.1
  46.2 0.7 %copy.18 = f32[1,1,47,1024]{3,2,1,0:T(8,128)} copy(f32[1,1,47,1024]{3,1,2,0:T(1,128)S(1)} %copy-done.1) | data formatting | bytes 385024
  47.0 1.3 %slice.3.fresh_ref = f32[8,128]{1,0:T(8,128)} slice(f32[40,128]{1,0:T(8,128)} %get-tuple-element.11.forcing_ref), slice={[32:40], [0:128]} | slice | bytes 8192 | tf_op jit(solution)/shard_map/slice | solution.py:252
  48.2 2.0 %shard_map.123 = (f32[48,1024]{1,0:T(8,128)}, f32[16,128]{1,0:T(8,128)}) custom-call(f32[48,1024]{1,0:T(8,128)} %bitcast.20, f32[47,1024]{1,0:T(8,128)} %bitcast.19, f32[40,128]{1,0:T(8,128)} %get-tuple-element.11.forcing_ref), custom_call_target="tpu_custom_call" | custom-call | flops 1966080 | bytes 589824 | tf_op jit(solution)/shard_map/pallas_call | solution.py:157
  50.2 0.0 collective-permute-done.got0_ref
  50.2 0.0 copy-start.3
  50.2 0.0 collective-permute-done.1.got1_ref
  50.2 0.0 copy-start.4
  50.2 0.6 copy-done.3
  50.8 0.0 copy-done.4
  50.8 2.5 %shard_map.124 = (f32[8,128]{1,0:T(8,128)}, f32[8,3,128]{2,1,0:T(4,128)}) custom-call(s32[1]{0:T(128)} %bitcast.1.odd_ref, f32[32,128]{1,0:T(8,128)} %copy-done.3, f32[32,128]{1,0:T(8,128)} %copy-done.4, f32[8,128]{1,0:T(8,128)} %bitcast.25, f32[8,128]{1,0:T(8,128)} %slice.3.fresh_ref, f32[48,128]{1,0:T(8,128)} %get-tuple-element.15.offs_ref, ...), custom_call_target="tpu_custom_call" | custom-call | tf_op jit(solution)/shard_map/pallas_call | solution.py:217
  53.3 11.0 %all_to_all.10 = f32[8,3,128]{2,1,0:T(4,128)S(1)} all-to-all(f32[8,3,128]{2,1,0:T(4,128)} %get-tuple-element.18), channel_id=1, replica_groups=mesh['comp'=8,'tile'=96] {'comp'}, dimensions={0} | all-to-all | bytes 24576 | tf_op jit(solution)/shard_map/all_to_all | solution.py:254
  64.3 0.6 copy.13
Async XLA Ops:
  0.6 18.9 %copy-start.2 = (s32[1,1,6,1024]{3,1,2,0:T(1,128)S(1)}, s32[1,1,6,1024]{3,1,2,0:T(1,128)}, u32[]{:S(2)}) copy-start(s32[1,1,6,1024]{3,1,2,0:T(1,128)} %param.18) | copy-start | bytes 73732
  0.6 45.6 %copy-start.1 = (f32[1,1,47,1024]{3,1,2,0:T(1,128)S(1)}, f32[1,1,47,1024]{3,1,2,0:T(1,128)}, u32[]{:S(2)}) copy-start(f32[1,1,47,1024]{3,1,2,0:T(1,128)} %param.16) | copy-start | bytes 577540
  6.8 21.8 %all-to-all-start = ((f32[8,64,128]{2,1,0:T(8,128)}), f32[8,64,128]{2,1,0:T(8,128)S(1)}, u32[]{:S(2)}, u32[]{:S(2)}) async-start(f32[8,64,128]{2,1,0:T(8,128)} %shard_map.121), calls=%async_computation | async-start | bytes 524288 | tf_op jit(solution)/shard_map/all_to_all | solution.py:242
  28.6 0.7 %copy-start = (f32[8,64,128]{2,1,0:T(8,128)}, f32[8,64,128]{2,1,0:T(8,128)S(1)}, u32[]{:S(2)}) copy-start(f32[8,64,128]{2,1,0:T(8,128)S(1)} %all-to-all-done.arrived_ref) | copy-start | bytes 786436
  31.3 18.9 %collective-permute-start = (f32[32,128]{1,0:T(8,128)}, f32[32,128]{1,0:T(8,128)S(1)}, u32[]{:S(2)}, u32[]{:S(2)}) collective-permute-start(f32[32,128]{1,0:T(8,128)} %get-tuple-element.13), channel_id=1, source_target_pairs={{0,1},{1,0},{2,3},{3,2},{4,5},{5,4},{6,7},{7,6},{8,9},{9,8},{10,11... | collective-permute-start | bytes 49160 | tf_op jit(solution)/shard_map/ppermute | solution.py:249
  33.2 17.0 %collective-permute-start.1 = (f32[32,128]{1,0:T(8,128)}, f32[32,128]{1,0:T(8,128)S(1)}, u32[]{:S(2)}, u32[]{:S(2)}) collective-permute-start(f32[32,128]{1,0:T(8,128)} %get-tuple-element.14), channel_id=1, source_target_pairs={{0,95},{1,2},{2,1},{3,4},{4,3},{5,6},{6,5},{7,8},{8,7},{9,10},{10,... | collective-permute-start | bytes 49160 | tf_op jit(solution)/shard_map/ppermute | solution.py:248
  50.2 0.6 copy-start.3
  50.2 0.6 copy-start.4

commit v2 on v1

v2 whole, which is shorter than its diff:
```python
import functools
import math

import jax
import jax.numpy as jnp
from jax import lax
from jax.experimental import pallas as pl
from jax.experimental.pallas import tpu as pltpu
from jax.sharding import PartitionSpec as P

SUB = 8
MIX = 4
LANES = 128
FIELDS = 5

heat_gain = 0.5
shortwave_gain = 0.5
wind_mixing = 0.15
relax_rate = 0.5
fresh_gain = 0.5


def shape_of(dims, dtype=jnp.float32):
    return jax.ShapeDtypeStruct(dims, dtype)


def limit(mib):
    return pltpu.CompilerParams(vmem_limit_bytes=mib << 20)


def cost(flops, moved):
    return pl.CostEstimate(flops=flops, bytes_accessed=moved, transcendentals=0)


VMEM = pl.BlockSpec(memory_space=pltpu.VMEM)
SMEM = pl.BlockSpec(memory_space=pltpu.SMEM)
ANY = pl.BlockSpec(memory_space=pl.ANY)


def terms_kernel(src_ref, cnt_ref, flux_ref, weight_ref, out_ref, blocks_ref, term_ref, held_ref, sems):
    groups, slots = weight_ref.shape[:2]
    copies = [
        pltpu.make_async_copy(weight_ref.at[d], held_ref.at[d], sems.at[d]) for d in range(groups)
    ]
    for copy in copies:
        copy.start()
    for b in range(blocks_ref.shape[0]):
        blocks_ref[b] = flux_ref[:, b * LANES : (b + 1) * LANES].astype(jnp.float32)
    lane = lax.broadcasted_iota(jnp.int32, (8, LANES), 1)
    zero = jnp.zeros((8, LANES), jnp.float32)
    rest = out_ref.shape[1] - FIELDS * slots
    for d in range(groups):
        copies[d].wait()
        for k in range(0, slots, 2):
            parts = []
            for i in (0, 1):
                block = blocks_ref[src_ref[0, 0, d, k + i]]
                parts.append(jnp.where(lane < cnt_ref[0, 0, d, k + i], block, zero))
            top = jnp.concatenate([parts[0], zero], axis=1)
            low = jnp.concatenate([zero, parts[1]], axis=1)
            lhs = jnp.concatenate([top, low], axis=0).astype(jnp.bfloat16)
            rhs = held_ref[d, k : k + 2].reshape(2 * LANES, LANES)
            term_ref[d, k * 8 : k * 8 + 16, :] = jnp.dot(
                lhs, rhs, preferred_element_type=jnp.float32
            )
        f = [term_ref[d, pl.ds(i, slots, stride=8), :] for i in range(8)]
        for i, x in enumerate((f[1], f[0] + f[7], f[2], f[3], f[5] - f[4] + f[6])):
            out_ref[d, i * slots : (i + 1) * slots] = x
        if rest:
            out_ref[d, FIELDS * slots :] = jnp.zeros((rest, LANES), jnp.float32)


def remap_terms(src, cnt, flux, weights):
    groups, slots = weights.shape[:2]
    rows = -(-FIELDS * slots // 8) * 8
    return pl.pallas_call(
        terms_kernel,
        in_specs=[SMEM, SMEM, VMEM, ANY],
        out_specs=VMEM,
        out_shape=shape_of((groups, rows, LANES)),
        scratch_shapes=[
            pltpu.VMEM((flux.shape[1] // LANES, 8, LANES), jnp.float32),
            pltpu.VMEM((groups, slots * 8, LANES), jnp.float32),
            pltpu.VMEM(weights.shape, weights.dtype),
            pltpu.SemaphoreType.DMA((groups,)),
        ],
    )(src, cnt, flux, weights)


def target_kernel(after_ref, dst_ref, out_ref, *, rows):
    groups, slots = dst_ref.shape
    dst = dst_ref[...]
    parts = [dst + 8 * f for f in range(FIELDS)]
    rest = rows - FIELDS * slots
    if rest:
        parts.append(jnp.full((groups, rest), -1, jnp.int32))
    ids = jnp.concatenate(parts, axis=1)
    line = jnp.concatenate([ids[c : c + 1, :] for c in range(groups)], axis=1)
    targets = lax.broadcasted_iota(jnp.int32, out_ref.shape, 0)
    hit = jnp.broadcast_to(line, out_ref.shape) == targets
    out_ref[...] = hit.astype(jnp.float32).astype(jnp.bfloat16)


def one_hot_targets(after, dst):
    groups, rows, _ = after.shape
    return pl.pallas_call(
        functools.partial(target_kernel, rows=rows),
        in_specs=[ANY, VMEM],
        out_specs=VMEM,
        out_shape=shape_of((48, groups * rows), jnp.bfloat16),
        cost_estimate=cost(1 << 20, 1 << 20),
        compiler_params=limit(4),
    )(after, dst)


def forcing_kernel(odd_ref, arrived_ref, onehot_ref, ssh_ref, off_ref, forcing_ref, pay0_ref, pay1_ref):
    onehot = onehot_ref[...]
    rest = arrived_ref[...].reshape(-1, LANES)
    total = None
    for _ in range(3):
        piece = rest.astype(jnp.bfloat16)
        part = jnp.dot(onehot, piece, preferred_element_type=jnp.float32)
        total = part if total is None else total + part
        rest = rest - piece.astype(jnp.float32)
    forcing_ref[...] = total[: FIELDS * 8]
    odd = odd_ref[0] == 1
    pieces = [ssh_ref[...], total[(FIELDS - 1) * 8 : FIELDS * 8]]
    pieces += [off_ref[j].astype(jnp.float32) for j in range(off_ref.shape[0])]
    for i, x in enumerate(pieces):
        pay0_ref[4 * i : 4 * i + 4, :] = jnp.where(odd, x[0:4], x[4:8])
        pay1_ref[4 * i : 4 * i + 4, :] = jnp.where(odd, x[4:8], x[0:4])


def forcing_and_halo(odd, arrived, onehot, ssh, offsets):
    pay = shape_of((4 * (2 + offsets.shape[0]), LANES))
    return pl.pallas_call(
        forcing_kernel,
        in_specs=[SMEM] + [VMEM] * 4,
        out_specs=[VMEM] * 3,
        out_shape=[shape_of((FIELDS * 8, LANES)), pay, pay],
        compiler_params=limit(4),
    )(odd, arrived, onehot, ssh, offsets)


def column_parts(forcing_ref):
    east, north = forcing_ref[16:24, :], forcing_ref[24:32, :]
    mixing = wind_mixing * jnp.tanh(jnp.sqrt(east * east + north * north))
    return shortwave_gain * forcing_ref[0:8, :], heat_gain * forcing_ref[8:16, :], mixing


def mix_levels(kappa_ref, forcing_ref, tile_ref, levels):
    short, top, mixing = column_parts(forcing_ref)
    heated, keff = [], []
    for level in range(levels):
        shallow = math.exp(-level / 4.0) - math.exp(-(level + 1.0) / 4.0)
        value = tile_ref[level * 8 : level * 8 + 8, :] + short * shallow
        heated.append(value + top if level == 0 else value)
        if level < levels - 1:
            keff.append(kappa_ref[level] + mixing * math.exp(-level / 4.0))
    for _ in range(MIX):
        above = None
        for level in range(levels):
            here = heated[level]
            if level < levels - 1:
                below = keff[level] * (heated[level + 1] - here)
                new = here + below
            else:
                new = here
            heated[level] = new if above is None else new - above
            above = below
    return heated


def permuted(x, row, col):
    out = jnp.zeros((8, LANES), jnp.float32)
    for s in range(8):
        out = jnp.where(row == s, pick(jnp.broadcast_to(x[s : s + 1, :], (8, LANES)), col), out)
    return out


def pick(x, idx):
    return jnp.take_along_axis(x, idx, axis=1, mode="promise_in_bounds")


def surface_kernel(temp_ref, kappa_ref, forcing_ref, perm_ref, out_ref, tile_ref):
    for b in range(8):
        tile_ref[pl.ds(b, 8, stride=8), :] = temp_ref[:, b * LANES : (b + 1) * LANES]
    heated = mix_levels(kappa_ref, forcing_ref, tile_ref, MIX + 3)
    perm = perm_ref[...]
    row, col = perm >> 7, perm & (LANES - 1)
    for f in (0, 1):
        out_ref[f] = permuted(heated[f], row, col)


def surface_rows(temp, kappa, forcing, perm):
    return pl.pallas_call(
        surface_kernel,
        grid=(1,),
        in_specs=[
            pl.BlockSpec((8, temp.shape[1]), lambda i: (0, 0)),
            pl.BlockSpec((8, 8, LANES), lambda i: (0, 0, 0)),
            pl.BlockSpec(forcing.shape, lambda i: (0, 0)),
            pl.BlockSpec(perm.shape, lambda i: (0, 0)),
        ],
        out_specs=pl.BlockSpec((2, 8, LANES), lambda i: (0, 0, 0)),
        out_shape=shape_of((2, 8, LANES)),
        scratch_shapes=[pltpu.VMEM((64, LANES), jnp.float32)],
        cost_estimate=cost(1 << 20, 1 << 20),
        compiler_params=limit(4),
    )(temp, kappa, forcing, perm)


def column_kernel(after_ref, temp_ref, kappa_ref, forcing_ref, mixed_ref, tile_ref):
    levels = temp_ref.shape[0]
    for b in range(8):
        tile_ref[pl.ds(b, levels, stride=8), :] = temp_ref[:, b * LANES : (b + 1) * LANES]
    heated = mix_levels(kappa_ref, forcing_ref, tile_ref, levels)
    for level in range(levels):
        tile_ref[level * 8 : level * 8 + 8, :] = heated[level]
    for b in range(8):
        mixed_ref[:, b * LANES : (b + 1) * LANES] = tile_ref[pl.ds(b, levels, stride=8), :]


def column_update(after, temp, kappa, forcing):
    return pl.pallas_call(
        column_kernel,
        in_specs=[ANY] + [VMEM] * 3,
        out_specs=VMEM,
        out_shape=shape_of(temp.shape),
        scratch_shapes=[pltpu.VMEM((temp.shape[0] * 8, LANES), jnp.float32)],
        cost_estimate=cost(1 << 22, 1 << 22),
        compiler_params=limit(4),
    )(after, temp, kappa, forcing)


def height_kernel(odd_ref, got0_ref, got1_ref, ssh_ref, forcing_ref, off_ref, top_ref, perm_ref, ssh_out, state_out):
    odd = odd_ref[0] == 1
    count = off_ref.shape[0]

    def extended(i, own):
        a, b = got0_ref[4 * i : 4 * i + 4, :], got1_ref[4 * i : 4 * i + 4, :]
        left, right = jnp.where(odd, a, b), jnp.where(odd, b, a)
        return jnp.concatenate([left, own, right], axis=0)

    eta = extended(0, ssh_ref[...])
    fresh = (fresh_gain / SUB) * extended(1, forcing_ref[(FIELDS - 1) * 8 :, :])
    lane = lax.broadcasted_iota(jnp.int32, (16, LANES), 1)
    places, crossing = [], []
    for j in range(count):
        target = lane + extended(2 + j, off_ref[j].astype(jnp.float32)).astype(jnp.int32)
        places.append(target & (LANES - 1))
        crossing.append((target < 0) | (target >= LANES))
    upper = lane >= LANES // 2
    for _ in range(SUB):
        beside = jnp.where(upper, pltpu.roll(eta, 1, 0), pltpu.roll(eta, 15, 0))
        halves = []
        for h in (0, 8):
            here, other = eta[h : h + 8], beside[h : h + 8]
            near = None
            for j in range(count):
                idx = places[j][h : h + 8]
                value = jnp.where(crossing[j][h : h + 8], pick(other, idx), pick(here, idx))
                near = value if near is None else near + value
            halves.append(near)
        average = jnp.concatenate(halves, axis=0) / 6.0
        eta = eta + relax_rate * (average - eta) + fresh
    height = eta[4:12]
    ssh_out[...] = height
    perm = perm_ref[...]
    out = permuted(height, perm >> 7, perm & (LANES - 1))
    for f, x in enumerate((top_ref[0], top_ref[1], out)):
        for d in range(8):
            state_out[d, f : f + 1, :] = x[d : d + 1]


def heights_and_state(odd, got0, got1, ssh, forcing, offs, top, perm):
    return pl.pallas_call(
        height_kernel,
        in_specs=[SMEM] + [VMEM] * 7,
        out_specs=[VMEM] * 2,
        out_shape=[shape_of((8, LANES)), shape_of((8, 3, LANES))],
        compiler_params=limit(4),
    )(odd, got0, got1, ssh, forcing, offs, top, perm)


def per_device(
    atm_flux,
    intersection_weight,
    src_block,
    dst_block,
    intersection_count,
    temp,
    kappa,
    ssh,
    nbr_offset,
    coupler_perm,
):
    tiles = lax.axis_size("tile")
    odd = (lax.axis_index("tile") % 2).astype(jnp.int32).reshape(1)
    height = ssh.reshape(8, LANES)
    perm = coupler_perm.reshape(8, LANES)
    temp, conduct = temp[0, 0], kappa.reshape(kappa.shape[2], 8, LANES)
    offsets = nbr_offset.reshape(nbr_offset.shape[2], 8, LANES)
    terms = remap_terms(src_block, intersection_count, atm_flux[0, 0], intersection_weight[0, 0])
    arrived = lax.all_to_all(terms, "comp", split_axis=0, concat_axis=0, tiled=True)
    onehot = one_hot_targets(terms, dst_block[0, 0])
    forcing, pay0, pay1 = forcing_and_halo(odd, arrived, onehot, height, offsets)
    inner = [(i, i ^ 1) for i in range(tiles)]
    outer = [(i, (i - 1 if i % 2 == 0 else i + 1) % tiles) for i in range(tiles)]
    got0 = lax.ppermute(pay0, "tile", inner)
    got1 = lax.ppermute(pay1, "tile", outer)
    top = surface_rows(temp, conduct, forcing, perm)
    height, state = heights_and_state(odd, got0, got1, height, forcing, offsets, top, perm)
    mixed = column_update(state, temp, conduct, forcing)
    relaid = lax.all_to_all(state, "comp", split_axis=0, concat_axis=0, tiled=True)
    coupler_state = relaid.transpose(1, 0, 2).reshape(1, 1, 3, -1)
    return (mixed[None, None], height.reshape(ssh.shape), coupler_state)


def solution(mesh):
    return jax.shard_map(
        per_device,
        mesh=mesh,
        in_specs=(
            P("comp", "tile", None, None),
            P("comp", "tile", None, None, None, None),
            P("comp", "tile", None, None),
            P("comp", "tile", None, None),
            P("comp", "tile", None, None),
            P("comp", "tile", None, None),
            P("comp", "tile", None, None),
            P("comp", "tile", None),
            P("comp", "tile", None, None),
            P("comp", "tile", None),
        ),
        out_specs=(
            P("comp", "tile", None, None),
            P("comp", "tile", None),
            P("comp", "tile", None, None),
        ),
        check_vma=False,
    )
```

time: 65.5 us -> 57.1 us (0.87)
  blocking collectives: 11 us -> 0 us
  waiting for transfers between devices: 8.43 us -> 14.7 us
  Pallas kernels: 12.5 us -> 7.27 us
  starting transfers between devices: 27.7 us -> 32.4 us
  local copies, waits for them, and re-layouts: 4.52 us -> 1.62 us
    all_to_all x1 -> x0, blocking collectives: 11 us -> none  [per_device(): lax.all_to_all(state, 'comp', split_axis=0, concat_axis=0, tiled=True)]
    all_to_all x0 -> x1, waiting for transfers between devices: none -> 5.49 us  [per_device(): lax.all_to_all(state, 'comp', split_axis=0, concat_axis=0, tiled=True)]
    pallas_call x4 -> x6, Pallas kernels: 12.5 us -> 7.27 us  [the longest x1 4.14 us: remap_terms(): pl.pallas_call(terms_kernel, in_specs=[SMEM, SMEM, VMEM, ANY], out_specs=...]
    all_to_all x0 -> x1, starting transfers between devices: none -> 4.68 us  [per_device(): lax.all_to_all(state, 'comp', split_axis=0, concat_axis=0, tiled=True)]
    unnamed x13 -> x15, local copies, waits for them, and re-layouts: 3.26 us -> 1.62 us
    slice x1 -> x0, local copies, waits for them, and re-layouts: 1.26 us -> none  [per_device(): forcing[(FIELDS - 1) * 8:]]
    ppermute x1, waiting for transfers between devices: 0.01 us -> 1.25 us  [per_device(): got1 = lax.ppermute(pay1, 'tile', outer)]
  transfers between devices with their start and end apart: 3 -> 4, of which waited for: 1 -> 3; matrix products, arithmetic and copies ran while one was open for 4% -> 0% of each run, Pallas kernels for 3% -> 2%
where the time goes in v2:
time: 57.1 us; the launch traced here: 56.7 us
  starting transfers between devices  32.4 us (57%)
  waiting for transfers between devices  14.7 us (26%)
  Pallas kernels  7.27 us (13%)
  local copies, waits for them, and re-layouts  1.62 us (3%)
  between operations  0.76 us (1%)
    ppermute x1, starting transfers between devices, per_device(): got1 = lax.ppermute(pay1, 'tile', outer)  13 us
    all_to_all x1, starting transfers between devices, per_device(): lax.all_to_all(terms, 'comp', split_axis=0, concat_axis=0, tiled=True)  12.8 us
    all_to_all x1, waiting for transfers between devices, per_device(): lax.all_to_all(terms, 'comp', split_axis=0, concat_axis=0, tiled=True)  7.91 us
    all_to_all x1, waiting for transfers between devices, per_device(): lax.all_to_all(state, 'comp', split_axis=0, concat_axis=0, tiled=True)  5.49 us
    all_to_all x1, starting transfers between devices, per_device(): lax.all_to_all(state, 'comp', split_axis=0, concat_axis=0, tiled=True)  4.68 us
    pallas_call x1, Pallas kernels, remap_terms(): pl.pallas_call(terms_kernel, in_specs=[SMEM, SMEM, VMEM, ANY], out_specs=...  4.14 us
    ppermute x1, starting transfers between devices, per_device(): got0 = lax.ppermute(pay0, 'tile', inner)  1.92 us
    pallas_call x1, Pallas kernels, heights_and_state(): pl.pallas_call(height_kernel, in_specs=[SMEM] + [VMEM] * 7, out_specs=[VM...  1.74 us
  transfers between devices with their start and end apart: 4, of which 3 were waited for; matrix products, arithmetic and copies ran while one was open for 0% of the time, Pallas kernels for 2%

profile of v2, /device:TPU:8, one launch (start us, length us, event | category | flops | bytes accessed | tf_op | source)
XLA Modules:
  0.0 56.7 jit_solution(14020697391851686773)
XLA Ops:
  0.6 0.0 copy-start.6
  0.6 0.0 copy-start.3
  0.7 0.0 copy-start.4
  0.7 0.0 copy-start.5
  0.7 0.0 copy-start.2
  0.7 0.0 copy-start.1
  0.7 4.1 %shard_map.121.after_ref = f32[8,64,128]{2,1,0:T(8,128)} custom-call(s32[1,1,8,12]{3,2,1,0:T(8,128)} %src_ref.1, s32[1,1,8,12]{3,2,1,0:T(8,128)} %cnt_ref.1, bf16[8,1024]{1,0:T(8,128)(2,1)} %bitcast.28, bf16[8,12,128,128]{3,2,1,0:T(8,128)(2,1)} %bitcast.25), custom_call_target="tpu_custom_call" | custom-call | tf_op jit(solution)/shard_map/pallas_call | solution.py:76
  4.8 12.8 %all-to-all-start = ((f32[8,64,128]{2,1,0:T(8,128)}), f32[8,64,128]{2,1,0:T(8,128)S(1)}, u32[]{:S(2)}, u32[]{:S(2)}) async-start(f32[8,64,128]{2,1,0:T(8,128)} %shard_map.121.after_ref), calls=%async_computation | async-start | bytes 524288 | tf_op jit(solution)/shard_map/all_to_all | solution.py:305
  17.6 0.0 copy-done.6
  17.6 0.0 copy-start
  17.6 1.0 %copy-done = f32[8,64,128]{2,1,0:T(8,128)S(1)} copy-done((f32[8,64,128]{2,1,0:T(8,128)S(1)}, f32[8,64,128]{2,1,0:T(8,128)}, u32[]{:S(2)}) %copy-start) | copy-done | bytes 262168
  18.6 0.2 shard_map.122.onehot_ref
  18.8 7.9 %all-to-all-done.arrived_ref = f32[8,64,128]{2,1,0:T(8,128)S(1)} async-done(((f32[8,64,128]{2,1,0:T(8,128)}), f32[8,64,128]{2,1,0:T(8,128)S(1)}, u32[]{:S(2)}, u32[]{:S(2)}) %all-to-all-start) | async-done | bytes 262176 | tf_op jit(solution)/shard_map/all_to_all | solution.py:305
  26.7 0.0 copy-done.3
  26.7 0.0 copy-done.4
  26.7 0.2 shard_map.123
  26.9 1.9 %collective-permute-start = (f32[32,128]{1,0:T(8,128)S(1)}, f32[32,128]{1,0:T(8,128)S(1)}, u32[]{:S(2)}, u32[]{:S(2)}) collective-permute-start(f32[32,128]{1,0:T(8,128)S(1)} %get-tuple-element.8), channel_id=1, source_target_pairs={{0,1},{1,0},{2,3},{3,2},{4,5},{5,4},{6,7},{7,6},{8,9},{9,8},{10,11... | collective-permute-start | bytes 49160 | tf_op jit(solution)/shard_map/ppermute | solution.py:310
  28.8 13.0 %collective-permute-start.1 = (f32[32,128]{1,0:T(8,128)S(1)}, f32[32,128]{1,0:T(8,128)S(1)}, u32[]{:S(2)}, u32[]{:S(2)}) collective-permute-start(f32[32,128]{1,0:T(8,128)S(1)} %get-tuple-element.9), channel_id=1, source_target_pairs={{0,95},{1,2},{2,1},{3,4},{4,3},{5,6},{6,5},{7,8},{8,7},{9,10},{10,... | collective-permute-start | bytes 49160 | tf_op jit(solution)/shard_map/ppermute | solution.py:311
  41.9 0.0 copy-done.5
  41.9 0.0 copy-done.2
  41.9 0.0 copy-done.1
  41.9 0.1 shard_map.124.top_ref
  42.0 0.0 collective-permute-done.got0_ref
  42.0 1.3 %collective-permute-done.1.got1_ref = f32[32,128]{1,0:T(8,128)S(1)} collective-permute-done((f32[32,128]{1,0:T(8,128)S(1)}, f32[32,128]{1,0:T(8,128)S(1)}, u32[]{:S(2)}, u32[]{:S(2)}) %collective-permute-start.1) | collective-permute-done | bytes 16416 | tf_op jit(solution)/shard_map/ppermute | solution.py:311
  43.3 1.7 %shard_map.125 = (f32[8,128]{1,0:T(8,128)}, f32[8,3,128]{2,1,0:T(4,128)}) custom-call(s32[1]{0:T(128)} %bitcast.odd_ref, f32[32,128]{1,0:T(8,128)S(1)} %collective-permute-done.got0_ref, f32[32,128]{1,0:T(8,128)S(1)} %collective-permute-done.1.got1_ref, f32[8,128]{1,0:T(8,128)S(1)} %bitcast.21, f32[40,128]{1,0:T(8,128)S(1)} %get-tuple-element.10.forcing_ref, ...), custom_call_target="tpu_custom_call" | custom-call | tf_op jit(solution)/shard_map/pallas_call | solution.py:277
  45.0 4.7 %all-to-all-start.1 = ((f32[8,3,128]{2,1,0:T(4,128)}), f32[8,3,128]{2,1,0:T(4,128)S(1)}, u32[]{:S(2)}, u32[]{:S(2)}) async-start(f32[8,3,128]{2,1,0:T(4,128)} %get-tuple-element.11.after_ref), calls=%async_computation.1 | async-start | bytes 32768 | tf_op jit(solution)/shard_map/all_to_all | solution.py:315
  49.7 0.9 %shard_map.126 = f32[48,1024]{1,0:T(8,128)} custom-call(f32[8,3,128]{2,1,0:T(4,128)} %get-tuple-element.11.after_ref, f32[48,1024]{1,0:T(8,128)S(1)} %bitcast.15, f32[47,8,128]{2,1,0:T(8,128)S(1)} %bitcast.17, f32[40,128]{1,0:T(8,128)S(1)} %get-tuple-element.10.forcing_ref), custom_call_target="tpu_custom_call" | custom-call | flops 4194304 | bytes 4194304 | tf_op jit(solution)/shard_map/pallas_call | solution.py:225
  50.6 5.5 %all-to-all-done.1 = f32[8,3,128]{2,1,0:T(4,128)S(1)} async-done(((f32[8,3,128]{2,1,0:T(4,128)}), f32[8,3,128]{2,1,0:T(4,128)S(1)}, u32[]{:S(2)}, u32[]{:S(2)}) %all-to-all-start.1) | async-done | bytes 12320 | tf_op jit(solution)/shard_map/all_to_all | solution.py:315
  56.1 0.6 %copy.13 = f32[1,1,3,1024]{3,1,2,0:T(1,128)} copy(f32[1,1,3,1024]{3,2,1,0:T(4,128)S(1)} %bitcast.27) | data formatting | bytes 24576
Async XLA Ops:
  0.6 17.0 %copy-start.6 = (s32[1,1,8,12]{3,2,1,0:T(8,128)S(1)}, s32[1,1,8,12]{3,2,1,0:T(8,128)}, u32[]{:S(2)}) copy-start(s32[1,1,8,12]{3,2,1,0:T(8,128)} %param.13) | copy-start | bytes 1156
  0.6 26.0 %copy-start.3 = (s32[1,1,6,1024]{3,1,2,0:T(1,128)S(1)}, s32[1,1,6,1024]{3,1,2,0:T(1,128)}, u32[]{:S(2)}) copy-start(s32[1,1,6,1024]{3,1,2,0:T(1,128)} %param.18) | copy-start | bytes 73732
  0.7 26.0 %copy-start.4 = (f32[1,1,1024]{2,1,0:T(1,128)S(1)}, f32[1,1,1024]{2,1,0:T(1,128)}, u32[]{:S(2)}) copy-start(f32[1,1,1024]{2,1,0:T(1,128)} %param.17) | copy-start | bytes 12292
  0.7 41.2 %copy-start.5 = (s32[1,1,1024]{2,1,0:T(1,128)S(1)}, s32[1,1,1024]{2,1,0:T(1,128)}, u32[]{:S(2)}) copy-start(s32[1,1,1024]{2,1,0:T(1,128)} %param.19) | copy-start | bytes 12292
  0.7 41.2 %copy-start.2 = (f32[1,1,47,1024]{3,1,2,0:T(1,128)S(1)}, f32[1,1,47,1024]{3,1,2,0:T(1,128)}, u32[]{:S(2)}) copy-start(f32[1,1,47,1024]{3,1,2,0:T(1,128)} %param.16) | copy-start | bytes 577540
  0.7 41.2 %copy-start.1 = (f32[1,1,48,1024]{3,2,1,0:T(8,128)S(1)}, f32[1,1,48,1024]{3,2,1,0:T(8,128)}, u32[]{:S(2)}) copy-start(f32[1,1,48,1024]{3,2,1,0:T(8,128)} %param.15) | copy-start | bytes 589828
  4.8 21.8 %all-to-all-start = ((f32[8,64,128]{2,1,0:T(8,128)}), f32[8,64,128]{2,1,0:T(8,128)S(1)}, u32[]{:S(2)}, u32[]{:S(2)}) async-start(f32[8,64,128]{2,1,0:T(8,128)} %shard_map.121.after_ref), calls=%async_computation | async-start | bytes 524288 | tf_op jit(solution)/shard_map/all_to_all | solution.py:305
  17.6 1.0 %copy-start = (f32[8,64,128]{2,1,0:T(8,128)S(1)}, f32[8,64,128]{2,1,0:T(8,128)}, u32[]{:S(2)}) copy-start(f32[8,64,128]{2,1,0:T(8,128)} %shard_map.121.after_ref) | copy-start | bytes 786436
  26.9 15.1 %collective-permute-start = (f32[32,128]{1,0:T(8,128)S(1)}, f32[32,128]{1,0:T(8,128)S(1)}, u32[]{:S(2)}, u32[]{:S(2)}) collective-permute-start(f32[32,128]{1,0:T(8,128)S(1)} %get-tuple-element.8), channel_id=1, source_target_pairs={{0,1},{1,0},{2,3},{3,2},{4,5},{5,4},{6,7},{7,6},{8,9},{9,8},{10,11... | collective-permute-start | bytes 49160 | tf_op jit(solution)/shard_map/ppermute | solution.py:310
  28.8 14.4 %collective-permute-start.1 = (f32[32,128]{1,0:T(8,128)S(1)}, f32[32,128]{1,0:T(8,128)S(1)}, u32[]{:S(2)}, u32[]{:S(2)}) collective-permute-start(f32[32,128]{1,0:T(8,128)S(1)} %get-tuple-element.9), channel_id=1, source_target_pairs={{0,95},{1,2},{2,1},{3,4},{4,3},{5,6},{6,5},{7,8},{8,7},{9,10},{10,... | collective-permute-start | bytes 49160 | tf_op jit(solution)/shard_map/ppermute | solution.py:311
  45.0 11.1 %all-to-all-start.1 = ((f32[8,3,128]{2,1,0:T(4,128)}), f32[8,3,128]{2,1,0:T(4,128)S(1)}, u32[]{:S(2)}, u32[]{:S(2)}) async-start(f32[8,3,128]{2,1,0:T(4,128)} %get-tuple-element.11.after_ref), calls=%async_computation.1 | async-start | bytes 32768 | tf_op jit(solution)/shard_map/all_to_all | solution.py:315

commit v3 on v2

--- a/solution.py
+++ b/solution.py
@@ -37,13 +37,26 @@
 ANY = pl.BlockSpec(memory_space=pl.ANY)
 
 
-def terms_kernel(src_ref, cnt_ref, flux_ref, weight_ref, out_ref, blocks_ref, term_ref, held_ref, sems):
-    groups, slots = weight_ref.shape[:2]
+def terms_kernel(
+    src_hbm, cnt_hbm, flux_hbm, weight_hbm, out_hbm,
+    src_ref, cnt_ref, flux_ref, blocks_ref, term_ref, held_ref, out_ref, sems, out_sems,
+):
+    groups, slots = weight_hbm.shape[:2]
+    first = [
+        pltpu.make_async_copy(src_hbm, src_ref, sems.at[groups]),
+        pltpu.make_async_copy(cnt_hbm, cnt_ref, sems.at[groups + 1]),
+        pltpu.make_async_copy(flux_hbm, flux_ref, sems.at[groups + 2]),
+    ]
     copies = [
-        pltpu.make_async_copy(weight_ref.at[d], held_ref.at[d], sems.at[d]) for d in range(groups)
+        pltpu.make_async_copy(weight_hbm.at[d], held_ref.at[d], sems.at[d]) for d in range(groups)
     ]
-    for copy in copies:
+    results = [
+        pltpu.make_async_copy(out_ref.at[d], out_hbm.at[d], out_sems.at[d]) for d in range(groups)
+    ]
+    for copy in first + copies:
         copy.start()
+    for copy in first:
+        copy.wait()
     for b in range(blocks_ref.shape[0]):
         blocks_ref[b] = flux_ref[:, b * LANES : (b + 1) * LANES].astype(jnp.float32)
     lane = lax.broadcasted_iota(jnp.int32, (8, LANES), 1)
@@ -68,6 +81,9 @@
             out_ref[d, i * slots : (i + 1) * slots] = x
         if rest:
             out_ref[d, FIELDS * slots :] = jnp.zeros((rest, LANES), jnp.float32)
+        results[d].start()
+    for result in results:
+        result.wait()
 
 
 def remap_terms(src, cnt, flux, weights):
@@ -75,13 +91,18 @@
     rows = -(-FIELDS * slots // 8) * 8
     return pl.pallas_call(
         terms_kernel,
-        in_specs=[SMEM, SMEM, VMEM, ANY],
-        out_specs=VMEM,
+        in_specs=[ANY] * 4,
+        out_specs=ANY,
         out_shape=shape_of((groups, rows, LANES)),
         scratch_shapes=[
+            pltpu.SMEM(src.shape, jnp.int32),
+            pltpu.SMEM(cnt.shape, jnp.int32),
+            pltpu.VMEM(flux.shape, flux.dtype),
             pltpu.VMEM((flux.shape[1] // LANES, 8, LANES), jnp.float32),
             pltpu.VMEM((groups, slots * 8, LANES), jnp.float32),
             pltpu.VMEM(weights.shape, weights.dtype),
+            pltpu.VMEM((groups, rows, LANES), jnp.float32),
+            pltpu.SemaphoreType.DMA((groups + 3,)),
             pltpu.SemaphoreType.DMA((groups,)),
         ],
     )(src, cnt, flux, weights)
@@ -113,7 +134,7 @@
     )(after, dst)
 
 
-def forcing_kernel(odd_ref, arrived_ref, onehot_ref, ssh_ref, off_ref, forcing_ref, pay0_ref, pay1_ref):
+def forcing_kernel(place_ref, arrived_ref, onehot_ref, ssh_ref, off_ref, forcing_ref, pay0_ref, pay1_ref, pay2_ref):
     onehot = onehot_ref[...]
     rest = arrived_ref[...].reshape(-1, LANES)
     total = None
@@ -123,23 +144,24 @@
         total = part if total is None else total + part
         rest = rest - piece.astype(jnp.float32)
     forcing_ref[...] = total[: FIELDS * 8]
-    odd = odd_ref[0] == 1
+    odd = place_ref[0] % 2 == 1
     pieces = [ssh_ref[...], total[(FIELDS - 1) * 8 : FIELDS * 8]]
     pieces += [off_ref[j].astype(jnp.float32) for j in range(off_ref.shape[0])]
     for i, x in enumerate(pieces):
         pay0_ref[4 * i : 4 * i + 4, :] = jnp.where(odd, x[0:4], x[4:8])
         pay1_ref[4 * i : 4 * i + 4, :] = jnp.where(odd, x[4:8], x[0:4])
-
-
-def forcing_and_halo(odd, arrived, onehot, ssh, offsets):
+        pay2_ref[4 * i : 4 * i + 4, :] = jnp.where(odd, x[0:4], x[4:8])
+
+
+def forcing_and_halo(place, arrived, onehot, ssh, offsets):
     pay = shape_of((4 * (2 + offsets.shape[0]), LANES))
     return pl.pallas_call(
         forcing_kernel,
         in_specs=[SMEM] + [VMEM] * 4,
-        out_specs=[VMEM] * 3,
-        out_shape=[shape_of((FIELDS * 8, LANES)), pay, pay],
-        compiler_params=limit(4),
-    )(odd, arrived, onehot, ssh, offsets)
+        out_specs=[VMEM] * 4,
+        out_shape=[shape_of((FIELDS * 8, LANES)), pay, pay, pay],
+        compiler_params=limit(4),
+    )(place, arrived, onehot, ssh, offsets)
 
 
 def column_parts(forcing_ref):
@@ -210,7 +232,8 @@
     )(temp, kappa, forcing, perm)
 
 
-def column_kernel(after_ref, temp_ref, kappa_ref, forcing_ref, mixed_ref, tile_ref):
+def column_kernel(height_ref, temp_ref, kappa_ref, forcing_ref, mixed_ref, ssh_out, tile_ref):
+    ssh_out[...] = height_ref[...]
     levels = temp_ref.shape[0]
     for b in range(8):
         tile_ref[pl.ds(b, levels, stride=8), :] = temp_ref[:, b * LANES : (b + 1) * LANES]
@@ -221,24 +244,25 @@
         mixed_ref[:, b * LANES : (b + 1) * LANES] = tile_ref[pl.ds(b, levels, stride=8), :]
 
 
-def column_update(after, temp, kappa, forcing):
+def column_update(height, temp, kappa, forcing):
     return pl.pallas_call(
         column_kernel,
-        in_specs=[ANY] + [VMEM] * 3,
-        out_specs=VMEM,
-        out_shape=shape_of(temp.shape),
+        in_specs=[VMEM] * 4,
+        out_specs=[VMEM] * 2,
+        out_shape=[shape_of(temp.shape), shape_of(height.shape)],
         scratch_shapes=[pltpu.VMEM((temp.shape[0] * 8, LANES), jnp.float32)],
         cost_estimate=cost(1 << 22, 1 << 22),
         compiler_params=limit(4),
-    )(after, temp, kappa, forcing)
-
-
-def height_kernel(odd_ref, got0_ref, got1_ref, ssh_ref, forcing_ref, off_ref, top_ref, perm_ref, ssh_out, state_out):
-    odd = odd_ref[0] == 1
+    )(height, temp, kappa, forcing)
+
+
+def height_kernel(place_ref, got0_ref, got1_ref, got2_ref, ssh_ref, forcing_ref, off_ref, top_ref, perm_ref, ssh_out, state_out):
+    odd, late = place_ref[0] % 2 == 1, place_ref[0] >= 2
     count = off_ref.shape[0]
 
     def extended(i, own):
-        a, b = got0_ref[4 * i : 4 * i + 4, :], got1_ref[4 * i : 4 * i + 4, :]
+        rows = slice(4 * i, 4 * i + 4)
+        a, b = jnp.where(late, got2_ref[rows, :], got0_ref[rows, :]), got1_ref[rows, :]
         left, right = jnp.where(odd, a, b), jnp.where(odd, b, a)
         return jnp.concatenate([left, own, right], axis=0)
 
@@ -252,18 +276,19 @@
         crossing.append((target < 0) | (target >= LANES))
     upper = lane >= LANES // 2
     for _ in range(SUB):
+        kept = (1.0 - relax_rate) * eta + fresh
         beside = jnp.where(upper, pltpu.roll(eta, 1, 0), pltpu.roll(eta, 15, 0))
         halves = []
         for h in (0, 8):
             here, other = eta[h : h + 8], beside[h : h + 8]
-            near = None
+            near = []
             for j in range(count):
                 idx = places[j][h : h + 8]
-                value = jnp.where(crossing[j][h : h + 8], pick(other, idx), pick(here, idx))
-                near = value if near is None else near + value
-            halves.append(near)
-        average = jnp.concatenate(halves, axis=0) / 6.0
-        eta = eta + relax_rate * (average - eta) + fresh
+                near.append(jnp.where(crossing[j][h : h + 8], pick(other, idx), pick(here, idx)))
+            while len(near) > 1:
+                near = [sum(near[i : i + 2]) for i in range(0, len(near), 2)]
+            halves.append(near[0])
+        eta = kept + (relax_rate / count) * jnp.concatenate(halves, axis=0)
     height = eta[4:12]
     ssh_out[...] = height
     perm = perm_ref[...]
@@ -273,14 +298,14 @@
             state_out[d, f : f + 1, :] = x[d : d + 1]
 
 
-def heights_and_state(odd, got0, got1, ssh, forcing, offs, top, perm):
+def heights_and_state(place, got0, got1, got2, ssh, forcing, offs, top, perm):
     return pl.pallas_call(
         height_kernel,
-        in_specs=[SMEM] + [VMEM] * 7,
+        in_specs=[SMEM] + [VMEM] * 8,
         out_specs=[VMEM] * 2,
-        out_shape=[shape_of((8, LANES)), shape_of((8, 3, LANES))],
-        compiler_params=limit(4),
-    )(odd, got0, got1, ssh, forcing, offs, top, perm)
+        out_shape=[pltpu.VMEM((8, LANES), jnp.float32), pltpu.VMEM((8, 3, LANES), jnp.float32)],
+        compiler_params=limit(4),
+    )(place, got0, got1, got2, ssh, forcing, offs, top, perm)
 
 
 def per_device(
@@ -296,7 +321,8 @@
     coupler_perm,
 ):
     tiles = lax.axis_size("tile")
-    odd = (lax.axis_index("tile") % 2).astype(jnp.int32).reshape(1)
+    tile = lax.axis_index("tile")
+    place = (tile % 2 + 2 * (tile % 24 >= 22)).astype(jnp.int32).reshape(1)
     height = ssh.reshape(8, LANES)
     perm = coupler_perm.reshape(8, LANES)
     temp, conduct = temp[0, 0], kappa.reshape(kappa.shape[2], 8, LANES)
@@ -304,14 +330,17 @@
     terms = remap_terms(src_block, intersection_count, atm_flux[0, 0], intersection_weight[0, 0])
     arrived = lax.all_to_all(terms, "comp", split_axis=0, concat_axis=0, tiled=True)
     onehot = one_hot_targets(terms, dst_block[0, 0])
-    forcing, pay0, pay1 = forcing_and_halo(odd, arrived, onehot, height, offsets)
-    inner = [(i, i ^ 1) for i in range(tiles)]
+    forcing, pay0, pay1, pay2 = forcing_and_halo(place, arrived, onehot, height, offsets)
+    late = [i for i in range(tiles) if i % 24 >= 22]
+    inner = [(i, i ^ 1) for i in range(tiles) if i not in late]
+    inner_late = [(i, i ^ 1) for i in late]
     outer = [(i, (i - 1 if i % 2 == 0 else i + 1) % tiles) for i in range(tiles)]
     got0 = lax.ppermute(pay0, "tile", inner)
     got1 = lax.ppermute(pay1, "tile", outer)
+    got2 = lax.ppermute(pay2, "tile", inner_late)
     top = surface_rows(temp, conduct, forcing, perm)
-    height, state = heights_and_state(odd, got0, got1, height, forcing, offsets, top, perm)
-    mixed = column_update(state, temp, conduct, forcing)
+    height, state = heights_and_state(place, got0, got1, got2, height, forcing, offsets, top, perm)
+    mixed, height = column_update(height, temp, conduct, forcing)
     relaid = lax.all_to_all(state, "comp", split_axis=0, concat_axis=0, tiled=True)
     coupler_state = relaid.transpose(1, 0, 2).reshape(1, 1, 3, -1)
     return (mixed[None, None], height.reshape(ssh.shape), coupler_state)

time: 57.1 us -> 52.4 us (0.918)
  starting transfers between devices: 32.4 us -> 29.4 us
  Pallas kernels: 7.27 us -> 6.35 us
  waiting for transfers between devices: 14.7 us -> 14 us
    ppermute x1, starting transfers between devices: 13 us -> 8.52 us  [per_device(): got1 = lax.ppermute(pay1, 'tile', outer)]
    pallas_call x3, Pallas kernels: 6.77 us -> 5.86 us  [the longest x1 3.29 us: remap_terms(): pl.pallas_call(terms_kernel, in_specs=[ANY] * 4, out_specs=ANY, out_shape...]
    all_to_all x1, starting transfers between devices: 4.68 us -> 5.46 us  [per_device(): lax.all_to_all(state, 'comp', split_axis=0, concat_axis=0, tiled=True)]
    ppermute x1, waiting for transfers between devices: 1.25 us -> 0.58 us  [per_device(): got1 = lax.ppermute(pay1, 'tile', outer)]
    ppermute x0 -> x1, starting transfers between devices: none -> 0.66 us  [per_device(): got2 = lax.ppermute(pay2, 'tile', inner_late)]
  transfers between devices with their start and end apart: 4 -> 5, of which waited for: 3 -> 3; matrix products, arithmetic and copies ran while one was open for 0% -> 0% of each run, Pallas kernels for 2% -> 2%
where the time goes in v3:
time: 52.4 us; the launch traced here: 52.1 us
  starting transfers between devices  29.4 us (56%)
  waiting for transfers between devices  14 us (27%)
  Pallas kernels  6.35 us (12%)
  local copies, waits for them, and re-layouts  1.62 us (3%)
  between operations  0.77 us (1%)
    all_to_all x1, starting transfers between devices, per_device(): lax.all_to_all(terms, 'comp', split_axis=0, concat_axis=0, tiled=True)  12.8 us
    ppermute x1, starting transfers between devices, per_device(): got1 = lax.ppermute(pay1, 'tile', outer)  8.52 us
    all_to_all x1, waiting for transfers between devices, per_device(): lax.all_to_all(terms, 'comp', split_axis=0, concat_axis=0, tiled=True)  7.91 us
    all_to_all x1, waiting for transfers between devices, per_device(): lax.all_to_all(state, 'comp', split_axis=0, concat_axis=0, tiled=True)  5.48 us
    all_to_all x1, starting transfers between devices, per_device(): lax.all_to_all(state, 'comp', split_axis=0, concat_axis=0, tiled=True)  5.46 us
    pallas_call x1, Pallas kernels, remap_terms(): pl.pallas_call(terms_kernel, in_specs=[ANY] * 4, out_specs=ANY, out_shape...  3.29 us
    ppermute x1, starting transfers between devices, per_device(): got0 = lax.ppermute(pay0, 'tile', inner)  1.92 us
    pallas_call x1, Pallas kernels, heights_and_state(): pl.pallas_call(height_kernel, in_specs=[SMEM] + [VMEM] * 8, out_specs=[VM...  1.67 us
  transfers between devices with their start and end apart: 5, of which 3 were waited for; matrix products, arithmetic and copies ran while one was open for 0% of the time, Pallas kernels for 2%

profile of v3, /device:TPU:8, one launch (start us, length us, event | category | flops | bytes accessed | tf_op | source)
XLA Modules:
  0.0 52.1 jit_solution(10116252029531832957)
XLA Ops:
  0.6 0.0 copy-start.6
  0.6 0.0 copy-start.3
  0.7 0.0 copy-start.4
  0.7 0.0 copy-start.5
  0.7 0.0 copy-start.2
  0.7 0.0 copy-start.1
  0.7 3.3 %shard_map.121.after_ref = f32[8,64,128]{2,1,0:T(8,128)} custom-call(s32[1,1,8,12]{3,2,1,0:T(8,128)} %src_hbm.1, s32[1,1,8,12]{3,2,1,0:T(8,128)} %cnt_hbm.1, bf16[8,1024]{1,0:T(8,128)(2,1)} %bitcast.27, bf16[8,12,128,128]{3,2,1,0:T(8,128)(2,1)} %bitcast.25), custom_call_target="tpu_custom_call" | custom-call | tf_op jit(solution)/shard_map/pallas_call | solution.py:92
  4.0 12.8 %all-to-all-start = ((f32[8,64,128]{2,1,0:T(8,128)}), f32[8,64,128]{2,1,0:T(8,128)S(1)}, u32[]{:S(2)}, u32[]{:S(2)}) async-start(f32[8,64,128]{2,1,0:T(8,128)} %shard_map.121.after_ref), calls=%async_computation | async-start | bytes 524288 | tf_op jit(solution)/shard_map/all_to_all | solution.py:331
  16.8 0.0 copy-done.6
  16.8 0.0 copy-start
  16.8 1.0 %copy-done = f32[8,64,128]{2,1,0:T(8,128)S(1)} copy-done((f32[8,64,128]{2,1,0:T(8,128)S(1)}, f32[8,64,128]{2,1,0:T(8,128)}, u32[]{:S(2)}) %copy-start) | copy-done | bytes 262168
  17.8 0.2 shard_map.122.onehot_ref
  17.9 7.9 %all-to-all-done.arrived_ref = f32[8,64,128]{2,1,0:T(8,128)S(1)} async-done(((f32[8,64,128]{2,1,0:T(8,128)}), f32[8,64,128]{2,1,0:T(8,128)S(1)}, u32[]{:S(2)}, u32[]{:S(2)}) %all-to-all-start) | async-done | bytes 262176 | tf_op jit(solution)/shard_map/all_to_all | solution.py:331
  25.8 0.0 copy-done.3
  25.8 0.0 copy-done.4
  25.8 0.2 shard_map.123
  26.1 1.9 %collective-permute-start = (f32[32,128]{1,0:T(8,128)S(1)}, f32[32,128]{1,0:T(8,128)S(1)}, u32[]{:S(2)}, u32[]{:S(2)}) collective-permute-start(f32[32,128]{1,0:T(8,128)S(1)} %get-tuple-element.11), channel_id=1, source_target_pairs={{0,1},{1,0},{2,3},{3,2},{4,5},{5,4},{6,7},{7,6},{8,9},{9,8},{10,11... | collective-permute-start | bytes 49160 | tf_op jit(solution)/shard_map/ppermute | solution.py:338
  28.0 8.5 %collective-permute-start.1 = (f32[32,128]{1,0:T(8,128)S(1)}, f32[32,128]{1,0:T(8,128)S(1)}, u32[]{:S(2)}, u32[]{:S(2)}) collective-permute-start(f32[32,128]{1,0:T(8,128)S(1)} %get-tuple-element.12), channel_id=1, source_target_pairs={{0,95},{1,2},{2,1},{3,4},{4,3},{5,6},{6,5},{7,8},{8,7},{9,10},{10,... | collective-permute-start | bytes 49160 | tf_op jit(solution)/shard_map/ppermute | solution.py:339
  36.5 0.7 %collective-permute-start.2 = (f32[32,128]{1,0:T(8,128)S(1)}, f32[32,128]{1,0:T(8,128)S(1)}, u32[]{:S(2)}, u32[]{:S(2)}) collective-permute-start(f32[32,128]{1,0:T(8,128)S(1)} %get-tuple-element.13), channel_id=1, source_target_pairs={{22,23},{23,22},{46,47},{47,46},{70,71},{71,70},{94,95},{95,94},{1... | collective-permute-start | bytes 49160 | tf_op jit(solution)/shard_map/ppermute | solution.py:340
  37.2 0.0 copy-done.5
  37.2 0.0 copy-done.2
  37.2 0.0 copy-done.1
  37.2 0.1 shard_map.124.top_ref
  37.3 0.0 collective-permute-done.got0_ref
  37.4 0.6 %collective-permute-done.1.got1_ref = f32[32,128]{1,0:T(8,128)S(1)} collective-permute-done((f32[32,128]{1,0:T(8,128)S(1)}, f32[32,128]{1,0:T(8,128)S(1)}, u32[]{:S(2)}, u32[]{:S(2)}) %collective-permute-start.1) | collective-permute-done | bytes 16416 | tf_op jit(solution)/shard_map/ppermute | solution.py:339
  37.9 0.0 collective-permute-done.2.got2_ref
  37.9 1.7 %shard_map.125 = (f32[8,128]{1,0:T(8,128)S(1)}, f32[8,3,128]{2,1,0:T(4,128)}) custom-call(s32[1]{0:T(128)} %bitcast.place_ref, f32[32,128]{1,0:T(8,128)S(1)} %collective-permute-done.got0_ref, f32[32,128]{1,0:T(8,128)S(1)} %collective-permute-done.1.got1_ref, f32[32,128]{1,0:T(8,128)S(1)} %collective-permute-done.2.got2_ref, f32[8,128]{1,0:T(8,128)S(1)} %bitcast.21, ...), custom_call_target="tpu_custom_call" | custom-call | tf_op jit(solution)/shard_map/pallas_call | solution.py:302
  39.6 5.5 %all-to-all-start.1 = ((f32[8,3,128]{2,1,0:T(4,128)}), f32[8,3,128]{2,1,0:T(4,128)S(1)}, u32[]{:S(2)}, u32[]{:S(2)}) async-start(f32[8,3,128]{2,1,0:T(4,128)} %get-tuple-element.18), calls=%async_computation.1 | async-start | bytes 32768 | tf_op jit(solution)/shard_map/all_to_all | solution.py:344
  45.1 0.9 %shard_map.126 = (f32[48,1024]{1,0:T(8,128)}, f32[8,128]{1,0:T(8,128)}) custom-call(f32[8,128]{1,0:T(8,128)S(1)} %get-tuple-element.15.height_ref, f32[48,1024]{1,0:T(8,128)S(1)} %bitcast.15, f32[47,8,128]{2,1,0:T(8,128)S(1)} %bitcast.17, f32[40,128]{1,0:T(8,128)S(1)} %get-tuple-element.14.forcing_ref), custom_call_target="tpu_custom_call" | custom-call | flops 4194304 | bytes 4194304 | tf_op jit(solution)/shard_map/pallas_call | solution.py:248
  46.0 5.5 %all-to-all-done.1 = f32[8,3,128]{2,1,0:T(4,128)S(1)} async-done(((f32[8,3,128]{2,1,0:T(4,128)}), f32[8,3,128]{2,1,0:T(4,128)S(1)}, u32[]{:S(2)}, u32[]{:S(2)}) %all-to-all-start.1) | async-done | bytes 12320 | tf_op jit(solution)/shard_map/all_to_all | solution.py:344
  51.5 0.6 %copy.13 = f32[1,1,3,1024]{3,1,2,0:T(1,128)} copy(f32[1,1,3,1024]{3,2,1,0:T(4,128)S(1)} %bitcast.26) | data formatting | bytes 24576
Async XLA Ops:
  0.6 16.1 %copy-start.6 = (s32[1,1,8,12]{3,2,1,0:T(8,128)S(1)}, s32[1,1,8,12]{3,2,1,0:T(8,128)}, u32[]{:S(2)}) copy-start(s32[1,1,8,12]{3,2,1,0:T(8,128)} %param.13) | copy-start | bytes 1156
  0.6 25.2 %copy-start.3 = (s32[1,1,6,1024]{3,1,2,0:T(1,128)S(1)}, s32[1,1,6,1024]{3,1,2,0:T(1,128)}, u32[]{:S(2)}) copy-start(s32[1,1,6,1024]{3,1,2,0:T(1,128)} %param.18) | copy-start | bytes 73732
  0.7 25.2 %copy-start.4 = (f32[1,1,1024]{2,1,0:T(1,128)S(1)}, f32[1,1,1024]{2,1,0:T(1,128)}, u32[]{:S(2)}) copy-start(f32[1,1,1024]{2,1,0:T(1,128)} %param.17) | copy-start | bytes 12292
  0.7 36.5 %copy-start.5 = (s32[1,1,1024]{2,1,0:T(1,128)S(1)}, s32[1,1,1024]{2,1,0:T(1,128)}, u32[]{:S(2)}) copy-start(s32[1,1,1024]{2,1,0:T(1,128)} %param.19) | copy-start | bytes 12292
  0.7 36.5 %copy-start.2 = (f32[1,1,47,1024]{3,1,2,0:T(1,128)S(1)}, f32[1,1,47,1024]{3,1,2,0:T(1,128)}, u32[]{:S(2)}) copy-start(f32[1,1,47,1024]{3,1,2,0:T(1,128)} %param.16) | copy-start | bytes 577540
  0.7 36.5 %copy-start.1 = (f32[1,1,48,1024]{3,2,1,0:T(8,128)S(1)}, f32[1,1,48,1024]{3,2,1,0:T(8,128)}, u32[]{:S(2)}) copy-start(f32[1,1,48,1024]{3,2,1,0:T(8,128)} %param.15) | copy-start | bytes 589828
  4.0 21.8 %all-to-all-start = ((f32[8,64,128]{2,1,0:T(8,128)}), f32[8,64,128]{2,1,0:T(8,128)S(1)}, u32[]{:S(2)}, u32[]{:S(2)}) async-start(f32[8,64,128]{2,1,0:T(8,128)} %shard_map.121.after_ref), calls=%async_computation | async-start | bytes 524288 | tf_op jit(solution)/shard_map/all_to_all | solution.py:331
  16.8 1.0 %copy-start = (f32[8,64,128]{2,1,0:T(8,128)S(1)}, f32[8,64,128]{2,1,0:T(8,128)}, u32[]{:S(2)}) copy-start(f32[8,64,128]{2,1,0:T(8,128)} %shard_map.121.after_ref) | copy-start | bytes 786436
  26.1 11.3 %collective-permute-start = (f32[32,128]{1,0:T(8,128)S(1)}, f32[32,128]{1,0:T(8,128)S(1)}, u32[]{:S(2)}, u32[]{:S(2)}) collective-permute-start(f32[32,128]{1,0:T(8,128)S(1)} %get-tuple-element.11), channel_id=1, source_target_pairs={{0,1},{1,0},{2,3},{3,2},{4,5},{5,4},{6,7},{7,6},{8,9},{9,8},{10,11... | collective-permute-start | bytes 49160 | tf_op jit(solution)/shard_map/ppermute | solution.py:338
  28.0 10.0 %collective-permute-start.1 = (f32[32,128]{1,0:T(8,128)S(1)}, f32[32,128]{1,0:T(8,128)S(1)}, u32[]{:S(2)}, u32[]{:S(2)}) collective-permute-start(f32[32,128]{1,0:T(8,128)S(1)} %get-tuple-element.12), channel_id=1, source_target_pairs={{0,95},{1,2},{2,1},{3,4},{4,3},{5,6},{6,5},{7,8},{8,7},{9,10},{10,... | collective-permute-start | bytes 49160 | tf_op jit(solution)/shard_map/ppermute | solution.py:339
  36.5 1.4 %collective-permute-start.2 = (f32[32,128]{1,0:T(8,128)S(1)}, f32[32,128]{1,0:T(8,128)S(1)}, u32[]{:S(2)}, u32[]{:S(2)}) collective-permute-start(f32[32,128]{1,0:T(8,128)S(1)} %get-tuple-element.13), channel_id=1, source_target_pairs={{22,23},{23,22},{46,47},{47,46},{70,71},{71,70},{94,95},{95,94},{1... | collective-permute-start | bytes 49160 | tf_op jit(solution)/shard_map/ppermute | solution.py:340
  39.6 11.8 %all-to-all-start.1 = ((f32[8,3,128]{2,1,0:T(4,128)}), f32[8,3,128]{2,1,0:T(4,128)S(1)}, u32[]{:S(2)}, u32[]{:S(2)}) async-start(f32[8,3,128]{2,1,0:T(4,128)} %get-tuple-element.18), calls=%async_computation.1 | async-start | bytes 32768 | tf_op jit(solution)/shard_map/all_to_all | solution.py:344

commit v4 on v3

--- a/solution.py
+++ b/solution.py
@@ -12,6 +12,8 @@
 MIX = 4
 LANES = 128
 FIELDS = 5
+TERMS_FIRST = 6
+STATE_FIRST = 4
 
 heat_gain = 0.5
 shortwave_gain = 0.5
@@ -22,6 +24,13 @@
 
 def shape_of(dims, dtype=jnp.float32):
     return jax.ShapeDtypeStruct(dims, dtype)
+
+
+def over_groups(x, groups, first):
+    order = [[(i + first) % groups for i in range(groups)]]
+    return lax.all_to_all(
+        x, "comp", split_axis=0, concat_axis=0, axis_index_groups=order, tiled=True
+    )
 
 
 def limit(mib):
@@ -51,7 +60,8 @@
         pltpu.make_async_copy(weight_hbm.at[d], held_ref.at[d], sems.at[d]) for d in range(groups)
     ]
     results = [
-        pltpu.make_async_copy(out_ref.at[d], out_hbm.at[d], out_sems.at[d]) for d in range(groups)
+        pltpu.make_async_copy(out_ref.at[d], out_hbm.at[(d - TERMS_FIRST) % groups], out_sems.at[d])
+        for d in range(groups)
     ]
     for copy in first + copies:
         copy.start()
@@ -116,7 +126,8 @@
     if rest:
         parts.append(jnp.full((groups, rest), -1, jnp.int32))
     ids = jnp.concatenate(parts, axis=1)
-    line = jnp.concatenate([ids[c : c + 1, :] for c in range(groups)], axis=1)
+    in_order = [(i + TERMS_FIRST) % groups for i in range(groups)]
+    line = jnp.concatenate([ids[c : c + 1, :] for c in in_order], axis=1)
     targets = lax.broadcasted_iota(jnp.int32, out_ref.shape, 0)
     hit = jnp.broadcast_to(line, out_ref.shape) == targets
     out_ref[...] = hit.astype(jnp.float32).astype(jnp.bfloat16)
@@ -295,7 +306,7 @@
     out = permuted(height, perm >> 7, perm & (LANES - 1))
     for f, x in enumerate((top_ref[0], top_ref[1], out)):
         for d in range(8):
-            state_out[d, f : f + 1, :] = x[d : d + 1]
+            state_out[(d - STATE_FIRST) % 8, f : f + 1, :] = x[d : d + 1]
 
 
 def heights_and_state(place, got0, got1, got2, ssh, forcing, offs, top, perm):
@@ -320,7 +331,7 @@
     nbr_offset,
     coupler_perm,
 ):
-    tiles = lax.axis_size("tile")
+    tiles, groups = lax.axis_size("tile"), lax.axis_size("comp")
     tile = lax.axis_index("tile")
     place = (tile % 2 + 2 * (tile % 24 >= 22)).astype(jnp.int32).reshape(1)
     height = ssh.reshape(8, LANES)
@@ -328,7 +339,7 @@
     temp, conduct = temp[0, 0], kappa.reshape(kappa.shape[2], 8, LANES)
     offsets = nbr_offset.reshape(nbr_offset.shape[2], 8, LANES)
     terms = remap_terms(src_block, intersection_count, atm_flux[0, 0], intersection_weight[0, 0])
-    arrived = lax.all_to_all(terms, "comp", split_axis=0, concat_axis=0, tiled=True)
+    arrived = over_groups(terms, groups, TERMS_FIRST)
     onehot = one_hot_targets(terms, dst_block[0, 0])
     forcing, pay0, pay1, pay2 = forcing_and_halo(place, arrived, onehot, height, offsets)
     late = [i for i in range(tiles) if i % 24 >= 22]
@@ -341,7 +352,8 @@
     top = surface_rows(temp, conduct, forcing, perm)
     height, state = heights_and_state(place, got0, got1, got2, height, forcing, offsets, top, perm)
     mixed, height = column_update(height, temp, conduct, forcing)
-    relaid = lax.all_to_all(state, "comp", split_axis=0, concat_axis=0, tiled=True)
+    relaid = over_groups(state, groups, STATE_FIRST)
+    relaid = jnp.roll(relaid, STATE_FIRST, axis=0)
     coupler_state = relaid.transpose(1, 0, 2).reshape(1, 1, 3, -1)
     return (mixed[None, None], height.reshape(ssh.shape), coupler_state)
 

time: 52.4 us -> 50 us (0.954)
  waiting for transfers between devices: 14 us -> 7.93 us
  starting transfers between devices: 29.4 us -> 32.9 us
    all_to_all x2, waiting for transfers between devices: 13.4 us -> 7.34 us  [over_groups(): lax.all_to_all(x, 'comp', split_axis=0, concat_axis=0, axis_index_groups=...]
    all_to_all x2, starting transfers between devices: 18.2 us -> 21 us  [over_groups(): lax.all_to_all(x, 'comp', split_axis=0, concat_axis=0, axis_index_groups=...]
    ppermute x1, starting transfers between devices: 8.52 us -> 9.34 us  [per_device(): got1 = lax.ppermute(pay1, 'tile', outer)]
where the time goes in v4:
time: 50 us; the launch traced here: 49.6 us
  starting transfers between devices  32.9 us (66%)
  waiting for transfers between devices  7.93 us (16%)
  Pallas kernels  6.36 us (13%)
  local copies, waits for them, and re-layouts  1.62 us (3%)
  between operations  0.77 us (2%)
    all_to_all x2, starting transfers between devices, over_groups(): lax.all_to_all(x, 'comp', split_axis=0, concat_axis=0, axis_index_groups=...  21 us
    ppermute x1, starting transfers between devices, per_device(): got1 = lax.ppermute(pay1, 'tile', outer)  9.34 us
    all_to_all x2, waiting for transfers between devices, over_groups(): lax.all_to_all(x, 'comp', split_axis=0, concat_axis=0, axis_index_groups=...  7.34 us
    pallas_call x1, Pallas kernels, remap_terms(): pl.pallas_call(terms_kernel, in_specs=[ANY] * 4, out_specs=ANY, out_shape...  3.3 us
    ppermute x1, starting transfers between devices, per_device(): got0 = lax.ppermute(pay0, 'tile', inner)  1.92 us
    pallas_call x1, Pallas kernels, heights_and_state(): pl.pallas_call(height_kernel, in_specs=[SMEM] + [VMEM] * 8, out_specs=[VM...  1.68 us
    unnamed x15, local copies, waits for them, and re-layouts  1.62 us
  transfers between devices with their start and end apart: 5, of which 3 were waited for; matrix products, arithmetic and copies ran while one was open for 0% of the time, Pallas kernels for 2%

profile of v4, /device:TPU:8, one launch (start us, length us, event | category | flops | bytes accessed | tf_op | source)
XLA Modules:
  0.0 49.6 jit_solution(12844601085355190508)
XLA Ops:
  0.6 0.0 copy-start.6
  0.6 0.0 copy-start.3
  0.7 0.0 copy-start.4
  0.7 0.0 copy-start.5
  0.7 0.0 copy-start.2
  0.7 0.0 copy-start.1
  0.7 3.3 %shard_map.121.after_ref = f32[8,64,128]{2,1,0:T(8,128)} custom-call(s32[1,1,8,12]{3,2,1,0:T(8,128)} %src_hbm.1, s32[1,1,8,12]{3,2,1,0:T(8,128)} %cnt_hbm.1, bf16[8,1024]{1,0:T(8,128)(2,1)} %bitcast.27, bf16[8,12,128,128]{3,2,1,0:T(8,128)(2,1)} %bitcast.26), custom_call_target="tpu_custom_call" | custom-call | tf_op jit(solution)/shard_map/pallas_call | solution.py:102
  4.0 14.3 %all-to-all-start = ((f32[8,64,128]{2,1,0:T(8,128)}), f32[8,64,128]{2,1,0:T(8,128)S(1)}, u32[]{:S(2)}, u32[]{:S(2)}) async-start(f32[8,64,128]{2,1,0:T(8,128)} %shard_map.121.after_ref), calls=%async_computation | async-start | bytes 524288 | tf_op jit(solution)/shard_map/all_to_all | solution.py:31
  18.3 0.0 copy-done.6
  18.3 0.0 copy-start
  18.3 1.0 %copy-done = f32[8,64,128]{2,1,0:T(8,128)S(1)} copy-done((f32[8,64,128]{2,1,0:T(8,128)S(1)}, f32[8,64,128]{2,1,0:T(8,128)}, u32[]{:S(2)}) %copy-start) | copy-done | bytes 262168
  19.3 0.2 shard_map.122.onehot_ref
  19.5 4.9 %all-to-all-done.arrived_ref = f32[8,64,128]{2,1,0:T(8,128)S(1)} async-done(((f32[8,64,128]{2,1,0:T(8,128)}), f32[8,64,128]{2,1,0:T(8,128)S(1)}, u32[]{:S(2)}, u32[]{:S(2)}) %all-to-all-start) | async-done | bytes 262176 | tf_op jit(solution)/shard_map/all_to_all | solution.py:31
  24.3 0.0 copy-done.3
  24.3 0.0 copy-done.4
  24.3 0.2 shard_map.123
  24.6 1.9 %collective-permute-start = (f32[32,128]{1,0:T(8,128)S(1)}, f32[32,128]{1,0:T(8,128)S(1)}, u32[]{:S(2)}, u32[]{:S(2)}) collective-permute-start(f32[32,128]{1,0:T(8,128)S(1)} %get-tuple-element.11), channel_id=1, source_target_pairs={{0,1},{1,0},{2,3},{3,2},{4,5},{5,4},{6,7},{7,6},{8,9},{9,8},{10,11... | collective-permute-start | bytes 49160 | tf_op jit(solution)/shard_map/ppermute | solution.py:349
  26.5 9.3 %collective-permute-start.1 = (f32[32,128]{1,0:T(8,128)S(1)}, f32[32,128]{1,0:T(8,128)S(1)}, u32[]{:S(2)}, u32[]{:S(2)}) collective-permute-start(f32[32,128]{1,0:T(8,128)S(1)} %get-tuple-element.12), channel_id=1, source_target_pairs={{0,95},{1,2},{2,1},{3,4},{4,3},{5,6},{6,5},{7,8},{8,7},{9,10},{10,... | collective-permute-start | bytes 49160 | tf_op jit(solution)/shard_map/ppermute | solution.py:350
  35.8 0.7 %collective-permute-start.2 = (f32[32,128]{1,0:T(8,128)S(1)}, f32[32,128]{1,0:T(8,128)S(1)}, u32[]{:S(2)}, u32[]{:S(2)}) collective-permute-start(f32[32,128]{1,0:T(8,128)S(1)} %get-tuple-element.13), channel_id=1, source_target_pairs={{22,23},{23,22},{46,47},{47,46},{70,71},{71,70},{94,95},{95,94},{1... | collective-permute-start | bytes 49160 | tf_op jit(solution)/shard_map/ppermute | solution.py:351
  36.5 0.0 copy-done.5
  36.5 0.0 copy-done.2
  36.5 0.0 copy-done.1
  36.5 0.1 shard_map.124.top_ref
  36.7 0.0 collective-permute-done.got0_ref
  36.7 0.6 %collective-permute-done.1.got1_ref = f32[32,128]{1,0:T(8,128)S(1)} collective-permute-done((f32[32,128]{1,0:T(8,128)S(1)}, f32[32,128]{1,0:T(8,128)S(1)}, u32[]{:S(2)}, u32[]{:S(2)}) %collective-permute-start.1) | collective-permute-done | bytes 16416 | tf_op jit(solution)/shard_map/ppermute | solution.py:350
  37.3 0.0 collective-permute-done.2.got2_ref
  37.3 1.7 %shard_map.125 = (f32[8,128]{1,0:T(8,128)S(1)}, f32[8,3,128]{2,1,0:T(4,128)}) custom-call(s32[1]{0:T(128)} %bitcast.place_ref, f32[32,128]{1,0:T(8,128)S(1)} %collective-permute-done.got0_ref, f32[32,128]{1,0:T(8,128)S(1)} %collective-permute-done.1.got1_ref, f32[32,128]{1,0:T(8,128)S(1)} %collective-permute-done.2.got2_ref, f32[8,128]{1,0:T(8,128)S(1)} %bitcast.22, ...), custom_call_target="tpu_custom_call" | custom-call | tf_op jit(solution)/shard_map/pallas_call | solution.py:313
  39.0 6.7 %all-to-all-start.1 = ((f32[8,3,128]{2,1,0:T(4,128)}), f32[8,3,128]{2,1,0:T(4,128)S(1)}, u32[]{:S(2)}, u32[]{:S(2)}) async-start(f32[8,3,128]{2,1,0:T(4,128)} %get-tuple-element.18), calls=%async_computation.1 | async-start | bytes 32768 | tf_op jit(solution)/shard_map/all_to_all | solution.py:31
  45.7 0.9 %shard_map.126 = (f32[48,1024]{1,0:T(8,128)}, f32[8,128]{1,0:T(8,128)}) custom-call(f32[8,128]{1,0:T(8,128)S(1)} %get-tuple-element.15.height_ref, f32[48,1024]{1,0:T(8,128)S(1)} %bitcast.16, f32[47,8,128]{2,1,0:T(8,128)S(1)} %bitcast.18, f32[40,128]{1,0:T(8,128)S(1)} %get-tuple-element.14.forcing_ref), custom_call_target="tpu_custom_call" | custom-call | flops 4194304 | bytes 4194304 | tf_op jit(solution)/shard_map/pallas_call | solution.py:259
  46.5 2.5 %all-to-all-done.1 = f32[8,3,128]{2,1,0:T(4,128)S(1)} async-done(((f32[8,3,128]{2,1,0:T(4,128)}), f32[8,3,128]{2,1,0:T(4,128)S(1)}, u32[]{:S(2)}, u32[]{:S(2)}) %all-to-all-start.1) | async-done | bytes 12320 | tf_op jit(solution)/shard_map/all_to_all | solution.py:31
  49.0 0.6 %copy.13 = f32[1,1,3,1024]{3,1,2,0:T(1,128)} copy(f32[1,1,3,1024]{3,2,1,0:T(4,128)S(1)} %maximum_bitcast_fusion) | data formatting | bytes 24576
  (2 shorter events, 0.0 us)
Async XLA Ops:
  0.6 17.7 %copy-start.6 = (s32[1,1,8,12]{3,2,1,0:T(8,128)S(1)}, s32[1,1,8,12]{3,2,1,0:T(8,128)}, u32[]{:S(2)}) copy-start(s32[1,1,8,12]{3,2,1,0:T(8,128)} %param.13) | copy-start | bytes 1156
  0.6 23.7 %copy-start.3 = (s32[1,1,6,1024]{3,1,2,0:T(1,128)S(1)}, s32[1,1,6,1024]{3,1,2,0:T(1,128)}, u32[]{:S(2)}) copy-start(s32[1,1,6,1024]{3,1,2,0:T(1,128)} %param.18) | copy-start | bytes 73732
  0.7 23.7 %copy-start.4 = (f32[1,1,1024]{2,1,0:T(1,128)S(1)}, f32[1,1,1024]{2,1,0:T(1,128)}, u32[]{:S(2)}) copy-start(f32[1,1,1024]{2,1,0:T(1,128)} %param.17) | copy-start | bytes 12292
  0.7 35.9 %copy-start.5 = (s32[1,1,1024]{2,1,0:T(1,128)S(1)}, s32[1,1,1024]{2,1,0:T(1,128)}, u32[]{:S(2)}) copy-start(s32[1,1,1024]{2,1,0:T(1,128)} %param.19) | copy-start | bytes 12292
  0.7 35.9 %copy-start.2 = (f32[1,1,47,1024]{3,1,2,0:T(1,128)S(1)}, f32[1,1,47,1024]{3,1,2,0:T(1,128)}, u32[]{:S(2)}) copy-start(f32[1,1,47,1024]{3,1,2,0:T(1,128)} %param.16) | copy-start | bytes 577540
  0.7 35.9 %copy-start.1 = (f32[1,1,48,1024]{3,2,1,0:T(8,128)S(1)}, f32[1,1,48,1024]{3,2,1,0:T(8,128)}, u32[]{:S(2)}) copy-start(f32[1,1,48,1024]{3,2,1,0:T(8,128)} %param.15) | copy-start | bytes 589828
  4.0 20.3 %all-to-all-start = ((f32[8,64,128]{2,1,0:T(8,128)}), f32[8,64,128]{2,1,0:T(8,128)S(1)}, u32[]{:S(2)}, u32[]{:S(2)}) async-start(f32[8,64,128]{2,1,0:T(8,128)} %shard_map.121.after_ref), calls=%async_computation | async-start | bytes 524288 | tf_op jit(solution)/shard_map/all_to_all | solution.py:31
  18.3 1.0 %copy-start = (f32[8,64,128]{2,1,0:T(8,128)S(1)}, f32[8,64,128]{2,1,0:T(8,128)}, u32[]{:S(2)}) copy-start(f32[8,64,128]{2,1,0:T(8,128)} %shard_map.121.after_ref) | copy-start | bytes 786436
  24.6 12.1 %collective-permute-start = (f32[32,128]{1,0:T(8,128)S(1)}, f32[32,128]{1,0:T(8,128)S(1)}, u32[]{:S(2)}, u32[]{:S(2)}) collective-permute-start(f32[32,128]{1,0:T(8,128)S(1)} %get-tuple-element.11), channel_id=1, source_target_pairs={{0,1},{1,0},{2,3},{3,2},{4,5},{5,4},{6,7},{7,6},{8,9},{9,8},{10,11... | collective-permute-start | bytes 49160 | tf_op jit(solution)/shard_map/ppermute | solution.py:349
  26.5 10.8 %collective-permute-start.1 = (f32[32,128]{1,0:T(8,128)S(1)}, f32[32,128]{1,0:T(8,128)S(1)}, u32[]{:S(2)}, u32[]{:S(2)}) collective-permute-start(f32[32,128]{1,0:T(8,128)S(1)} %get-tuple-element.12), channel_id=1, source_target_pairs={{0,95},{1,2},{2,1},{3,4},{4,3},{5,6},{6,5},{7,8},{8,7},{9,10},{10,... | collective-permute-start | bytes 49160 | tf_op jit(solution)/shard_map/ppermute | solution.py:350
  35.8 1.4 %collective-permute-start.2 = (f32[32,128]{1,0:T(8,128)S(1)}, f32[32,128]{1,0:T(8,128)S(1)}, u32[]{:S(2)}, u32[]{:S(2)}) collective-permute-start(f32[32,128]{1,0:T(8,128)S(1)} %get-tuple-element.13), channel_id=1, source_target_pairs={{22,23},{23,22},{46,47},{47,46},{70,71},{71,70},{94,95},{95,94},{1... | collective-permute-start | bytes 49160 | tf_op jit(solution)/shard_map/ppermute | solution.py:351
  39.0 10.1 %all-to-all-start.1 = ((f32[8,3,128]{2,1,0:T(4,128)}), f32[8,3,128]{2,1,0:T(4,128)S(1)}, u32[]{:S(2)}, u32[]{:S(2)}) async-start(f32[8,3,128]{2,1,0:T(4,128)} %get-tuple-element.18), calls=%async_computation.1 | async-start | bytes 32768 | tf_op jit(solution)/shard_map/all_to_all | solution.py:31

commit v5 on v4

--- a/solution.py
+++ b/solution.py
@@ -109,7 +109,7 @@
             pltpu.SMEM(cnt.shape, jnp.int32),
             pltpu.VMEM(flux.shape, flux.dtype),
             pltpu.VMEM((flux.shape[1] // LANES, 8, LANES), jnp.float32),
-            pltpu.VMEM((groups, slots * 8, LANES), jnp.float32),
+            pltpu.VMEM((groups, slots * 8 + 8, LANES), jnp.float32),
             pltpu.VMEM(weights.shape, weights.dtype),
             pltpu.VMEM((groups, rows, LANES), jnp.float32),
             pltpu.SemaphoreType.DMA((groups + 3,)),
@@ -237,7 +237,7 @@
         ],
         out_specs=pl.BlockSpec((2, 8, LANES), lambda i: (0, 0, 0)),
         out_shape=shape_of((2, 8, LANES)),
-        scratch_shapes=[pltpu.VMEM((64, LANES), jnp.float32)],
+        scratch_shapes=[pltpu.VMEM((72, LANES), jnp.float32)],
         cost_estimate=cost(1 << 20, 1 << 20),
         compiler_params=limit(4),
     )(temp, kappa, forcing, perm)
@@ -261,7 +261,7 @@
         in_specs=[VMEM] * 4,
         out_specs=[VMEM] * 2,
         out_shape=[shape_of(temp.shape), shape_of(height.shape)],
-        scratch_shapes=[pltpu.VMEM((temp.shape[0] * 8, LANES), jnp.float32)],
+        scratch_shapes=[pltpu.VMEM((temp.shape[0] * 8 + 8, LANES), jnp.float32)],
         cost_estimate=cost(1 << 22, 1 << 22),
         compiler_params=limit(4),
     )(height, temp, kappa, forcing)

time: 50 us -> 50 us (level)
  no operation moved by 1% of the time
where the time goes in v5:
time: 50 us; the launch traced here: 49.6 us
  starting transfers between devices  32.9 us (66%)
  waiting for transfers between devices  7.93 us (16%)
  Pallas kernels  6.36 us (13%)
  local copies, waits for them, and re-layouts  1.62 us (3%)
  between operations  0.77 us (2%)
    all_to_all x2, starting transfers between devices, over_groups(): lax.all_to_all(x, 'comp', split_axis=0, concat_axis=0, axis_index_groups=...  21 us
    ppermute x1, starting transfers between devices, per_device(): got1 = lax.ppermute(pay1, 'tile', outer)  9.35 us
    all_to_all x2, waiting for transfers between devices, over_groups(): lax.all_to_all(x, 'comp', split_axis=0, concat_axis=0, axis_index_groups=...  7.34 us
    pallas_call x1, Pallas kernels, remap_terms(): pl.pallas_call(terms_kernel, in_specs=[ANY] * 4, out_specs=ANY, out_shape...  3.29 us
    ppermute x1, starting transfers between devices, per_device(): got0 = lax.ppermute(pay0, 'tile', inner)  1.92 us
    pallas_call x1, Pallas kernels, heights_and_state(): pl.pallas_call(height_kernel, in_specs=[SMEM] + [VMEM] * 8, out_specs=[VM...  1.68 us
    unnamed x15, local copies, waits for them, and re-layouts  1.62 us
  transfers between devices with their start and end apart: 5, of which 3 were waited for; matrix products, arithmetic and copies ran while one was open for 0% of the time, Pallas kernels for 2%

profile of v5, /device:TPU:8, one launch (start us, length us, event | category | flops | bytes accessed | tf_op | source)
XLA Modules:
  0.0 49.6 jit_solution(2098229917005650721)
XLA Ops:
  0.6 0.0 copy-start.6
  0.6 0.0 copy-start.3
  0.7 0.0 copy-start.4
  0.7 0.0 copy-start.5
  0.7 0.0 copy-start.2
  0.7 0.0 copy-start.1
  0.7 3.3 %shard_map.121.after_ref = f32[8,64,128]{2,1,0:T(8,128)} custom-call(s32[1,1,8,12]{3,2,1,0:T(8,128)} %src_hbm.1, s32[1,1,8,12]{3,2,1,0:T(8,128)} %cnt_hbm.1, bf16[8,1024]{1,0:T(8,128)(2,1)} %bitcast.27, bf16[8,12,128,128]{3,2,1,0:T(8,128)(2,1)} %bitcast.26), custom_call_target="tpu_custom_call" | custom-call | tf_op jit(solution)/shard_map/pallas_call | solution.py:102
  4.0 14.3 %all-to-all-start = ((f32[8,64,128]{2,1,0:T(8,128)}), f32[8,64,128]{2,1,0:T(8,128)S(1)}, u32[]{:S(2)}, u32[]{:S(2)}) async-start(f32[8,64,128]{2,1,0:T(8,128)} %shard_map.121.after_ref), calls=%async_computation | async-start | bytes 524288 | tf_op jit(solution)/shard_map/all_to_all | solution.py:31
  18.3 0.0 copy-done.6
  18.3 0.0 copy-start
  18.3 1.0 %copy-done = f32[8,64,128]{2,1,0:T(8,128)S(1)} copy-done((f32[8,64,128]{2,1,0:T(8,128)S(1)}, f32[8,64,128]{2,1,0:T(8,128)}, u32[]{:S(2)}) %copy-start) | copy-done | bytes 262168
  19.3 0.2 shard_map.122.onehot_ref
  19.5 4.9 %all-to-all-done.arrived_ref = f32[8,64,128]{2,1,0:T(8,128)S(1)} async-done(((f32[8,64,128]{2,1,0:T(8,128)}), f32[8,64,128]{2,1,0:T(8,128)S(1)}, u32[]{:S(2)}, u32[]{:S(2)}) %all-to-all-start) | async-done | bytes 262176 | tf_op jit(solution)/shard_map/all_to_all | solution.py:31
  24.3 0.0 copy-done.3
  24.3 0.0 copy-done.4
  24.3 0.2 shard_map.123
  24.6 1.9 %collective-permute-start = (f32[32,128]{1,0:T(8,128)S(1)}, f32[32,128]{1,0:T(8,128)S(1)}, u32[]{:S(2)}, u32[]{:S(2)}) collective-permute-start(f32[32,128]{1,0:T(8,128)S(1)} %get-tuple-element.11), channel_id=1, source_target_pairs={{0,1},{1,0},{2,3},{3,2},{4,5},{5,4},{6,7},{7,6},{8,9},{9,8},{10,11... | collective-permute-start | bytes 49160 | tf_op jit(solution)/shard_map/ppermute | solution.py:349
  26.5 9.3 %collective-permute-start.1 = (f32[32,128]{1,0:T(8,128)S(1)}, f32[32,128]{1,0:T(8,128)S(1)}, u32[]{:S(2)}, u32[]{:S(2)}) collective-permute-start(f32[32,128]{1,0:T(8,128)S(1)} %get-tuple-element.12), channel_id=1, source_target_pairs={{0,95},{1,2},{2,1},{3,4},{4,3},{5,6},{6,5},{7,8},{8,7},{9,10},{10,... | collective-permute-start | bytes 49160 | tf_op jit(solution)/shard_map/ppermute | solution.py:350
  35.8 0.7 %collective-permute-start.2 = (f32[32,128]{1,0:T(8,128)S(1)}, f32[32,128]{1,0:T(8,128)S(1)}, u32[]{:S(2)}, u32[]{:S(2)}) collective-permute-start(f32[32,128]{1,0:T(8,128)S(1)} %get-tuple-element.13), channel_id=1, source_target_pairs={{22,23},{23,22},{46,47},{47,46},{70,71},{71,70},{94,95},{95,94},{1... | collective-permute-start | bytes 49160 | tf_op jit(solution)/shard_map/ppermute | solution.py:351
  36.5 0.0 copy-done.5
  36.5 0.0 copy-done.2
  36.5 0.0 copy-done.1
  36.5 0.1 shard_map.124.top_ref
  36.7 0.0 collective-permute-done.got0_ref
  36.7 0.6 %collective-permute-done.1.got1_ref = f32[32,128]{1,0:T(8,128)S(1)} collective-permute-done((f32[32,128]{1,0:T(8,128)S(1)}, f32[32,128]{1,0:T(8,128)S(1)}, u32[]{:S(2)}, u32[]{:S(2)}) %collective-permute-start.1) | collective-permute-done | bytes 16416 | tf_op jit(solution)/shard_map/ppermute | solution.py:350
  37.3 0.0 collective-permute-done.2.got2_ref
  37.3 1.7 %shard_map.125 = (f32[8,128]{1,0:T(8,128)S(1)}, f32[8,3,128]{2,1,0:T(4,128)}) custom-call(s32[1]{0:T(128)} %bitcast.place_ref, f32[32,128]{1,0:T(8,128)S(1)} %collective-permute-done.got0_ref, f32[32,128]{1,0:T(8,128)S(1)} %collective-permute-done.1.got1_ref, f32[32,128]{1,0:T(8,128)S(1)} %collective-permute-done.2.got2_ref, f32[8,128]{1,0:T(8,128)S(1)} %bitcast.22, ...), custom_call_target="tpu_custom_call" | custom-call | tf_op jit(solution)/shard_map/pallas_call | solution.py:313
  39.0 6.7 %all-to-all-start.1 = ((f32[8,3,128]{2,1,0:T(4,128)}), f32[8,3,128]{2,1,0:T(4,128)S(1)}, u32[]{:S(2)}, u32[]{:S(2)}) async-start(f32[8,3,128]{2,1,0:T(4,128)} %get-tuple-element.18), calls=%async_computation.1 | async-start | bytes 32768 | tf_op jit(solution)/shard_map/all_to_all | solution.py:31
  45.7 0.9 %shard_map.126 = (f32[48,1024]{1,0:T(8,128)}, f32[8,128]{1,0:T(8,128)}) custom-call(f32[8,128]{1,0:T(8,128)S(1)} %get-tuple-element.15.height_ref, f32[48,1024]{1,0:T(8,128)S(1)} %bitcast.16, f32[47,8,128]{2,1,0:T(8,128)S(1)} %bitcast.18, f32[40,128]{1,0:T(8,128)S(1)} %get-tuple-element.14.forcing_ref), custom_call_target="tpu_custom_call" | custom-call | flops 4194304 | bytes 4194304 | tf_op jit(solution)/shard_map/pallas_call | solution.py:259
  46.5 2.5 %all-to-all-done.1 = f32[8,3,128]{2,1,0:T(4,128)S(1)} async-done(((f32[8,3,128]{2,1,0:T(4,128)}), f32[8,3,128]{2,1,0:T(4,128)S(1)}, u32[]{:S(2)}, u32[]{:S(2)}) %all-to-all-start.1) | async-done | bytes 12320 | tf_op jit(solution)/shard_map/all_to_all | solution.py:31
  49.0 0.6 %copy.13 = f32[1,1,3,1024]{3,1,2,0:T(1,128)} copy(f32[1,1,3,1024]{3,2,1,0:T(4,128)S(1)} %maximum_bitcast_fusion) | data formatting | bytes 24576
  (2 shorter events, 0.0 us)
Async XLA Ops:
  0.6 17.7 %copy-start.6 = (s32[1,1,8,12]{3,2,1,0:T(8,128)S(1)}, s32[1,1,8,12]{3,2,1,0:T(8,128)}, u32[]{:S(2)}) copy-start(s32[1,1,8,12]{3,2,1,0:T(8,128)} %param.13) | copy-start | bytes 1156
  0.6 23.7 %copy-start.3 = (s32[1,1,6,1024]{3,1,2,0:T(1,128)S(1)}, s32[1,1,6,1024]{3,1,2,0:T(1,128)}, u32[]{:S(2)}) copy-start(s32[1,1,6,1024]{3,1,2,0:T(1,128)} %param.18) | copy-start | bytes 73732
  0.7 23.7 %copy-start.4 = (f32[1,1,1024]{2,1,0:T(1,128)S(1)}, f32[1,1,1024]{2,1,0:T(1,128)}, u32[]{:S(2)}) copy-start(f32[1,1,1024]{2,1,0:T(1,128)} %param.17) | copy-start | bytes 12292
  0.7 35.9 %copy-start.5 = (s32[1,1,1024]{2,1,0:T(1,128)S(1)}, s32[1,1,1024]{2,1,0:T(1,128)}, u32[]{:S(2)}) copy-start(s32[1,1,1024]{2,1,0:T(1,128)} %param.19) | copy-start | bytes 12292
  0.7 35.9 %copy-start.2 = (f32[1,1,47,1024]{3,1,2,0:T(1,128)S(1)}, f32[1,1,47,1024]{3,1,2,0:T(1,128)}, u32[]{:S(2)}) copy-start(f32[1,1,47,1024]{3,1,2,0:T(1,128)} %param.16) | copy-start | bytes 577540
  0.7 35.9 %copy-start.1 = (f32[1,1,48,1024]{3,2,1,0:T(8,128)S(1)}, f32[1,1,48,1024]{3,2,1,0:T(8,128)}, u32[]{:S(2)}) copy-start(f32[1,1,48,1024]{3,2,1,0:T(8,128)} %param.15) | copy-start | bytes 589828
  4.0 20.3 %all-to-all-start = ((f32[8,64,128]{2,1,0:T(8,128)}), f32[8,64,128]{2,1,0:T(8,128)S(1)}, u32[]{:S(2)}, u32[]{:S(2)}) async-start(f32[8,64,128]{2,1,0:T(8,128)} %shard_map.121.after_ref), calls=%async_computation | async-start | bytes 524288 | tf_op jit(solution)/shard_map/all_to_all | solution.py:31
  18.3 1.0 %copy-start = (f32[8,64,128]{2,1,0:T(8,128)S(1)}, f32[8,64,128]{2,1,0:T(8,128)}, u32[]{:S(2)}) copy-start(f32[8,64,128]{2,1,0:T(8,128)} %shard_map.121.after_ref) | copy-start | bytes 786436
  24.6 12.1 %collective-permute-start = (f32[32,128]{1,0:T(8,128)S(1)}, f32[32,128]{1,0:T(8,128)S(1)}, u32[]{:S(2)}, u32[]{:S(2)}) collective-permute-start(f32[32,128]{1,0:T(8,128)S(1)} %get-tuple-element.11), channel_id=1, source_target_pairs={{0,1},{1,0},{2,3},{3,2},{4,5},{5,4},{6,7},{7,6},{8,9},{9,8},{10,11... | collective-permute-start | bytes 49160 | tf_op jit(solution)/shard_map/ppermute | solution.py:349
  26.5 10.8 %collective-permute-start.1 = (f32[32,128]{1,0:T(8,128)S(1)}, f32[32,128]{1,0:T(8,128)S(1)}, u32[]{:S(2)}, u32[]{:S(2)}) collective-permute-start(f32[32,128]{1,0:T(8,128)S(1)} %get-tuple-element.12), channel_id=1, source_target_pairs={{0,95},{1,2},{2,1},{3,4},{4,3},{5,6},{6,5},{7,8},{8,7},{9,10},{10,... | collective-permute-start | bytes 49160 | tf_op jit(solution)/shard_map/ppermute | solution.py:350
  35.8 1.4 %collective-permute-start.2 = (f32[32,128]{1,0:T(8,128)S(1)}, f32[32,128]{1,0:T(8,128)S(1)}, u32[]{:S(2)}, u32[]{:S(2)}) collective-permute-start(f32[32,128]{1,0:T(8,128)S(1)} %get-tuple-element.13), channel_id=1, source_target_pairs={{22,23},{23,22},{46,47},{47,46},{70,71},{71,70},{94,95},{95,94},{1... | collective-permute-start | bytes 49160 | tf_op jit(solution)/shard_map/ppermute | solution.py:351
  39.0 10.1 %all-to-all-start.1 = ((f32[8,3,128]{2,1,0:T(4,128)}), f32[8,3,128]{2,1,0:T(4,128)S(1)}, u32[]{:S(2)}, u32[]{:S(2)}) async-start(f32[8,3,128]{2,1,0:T(4,128)} %get-tuple-element.18), calls=%async_computation.1 | async-start | bytes 32768 | tf_op jit(solution)/shard_map/all_to_all | solution.py:31

commit v6 on v5

--- a/solution.py
+++ b/solution.py
@@ -73,7 +73,9 @@
     zero = jnp.zeros((8, LANES), jnp.float32)
     rest = out_ref.shape[1] - FIELDS * slots
     for d in range(groups):
-        copies[d].wait()
+        if d % 2 == 0:
+            for copy in copies[d : d + 2]:
+                copy.wait()
         for k in range(0, slots, 2):
             parts = []
             for i in (0, 1):
@@ -91,7 +93,9 @@
             out_ref[d, i * slots : (i + 1) * slots] = x
         if rest:
             out_ref[d, FIELDS * slots :] = jnp.zeros((rest, LANES), jnp.float32)
-        results[d].start()
+        if d % 2 == 1 or d == groups - 1:
+            for result in results[d - d % 2 : d + 1]:
+                result.start()
     for result in results:
         result.wait()
 

time: 50 us -> 49.7 us (level)
  no operation moved by 1% of the time
where the time goes in v6:
time: 49.7 us; the launch traced here: 49.3 us
  starting transfers between devices  33 us (66%)
  waiting for transfers between devices  7.93 us (16%)
  Pallas kernels  5.99 us (12%)
  local copies, waits for them, and re-layouts  1.62 us (3%)
  between operations  0.77 us (2%)
    all_to_all x2, starting transfers between devices, over_groups(): lax.all_to_all(x, 'comp', split_axis=0, concat_axis=0, axis_index_groups=...  21 us
    ppermute x1, starting transfers between devices, per_device(): got1 = lax.ppermute(pay1, 'tile', outer)  9.35 us
    all_to_all x2, waiting for transfers between devices, over_groups(): lax.all_to_all(x, 'comp', split_axis=0, concat_axis=0, axis_index_groups=...  7.34 us
    pallas_call x1, Pallas kernels, remap_terms(): pl.pallas_call(terms_kernel, in_specs=[ANY] * 4, out_specs=ANY, out_shape...  2.92 us
    ppermute x1, starting transfers between devices, per_device(): got0 = lax.ppermute(pay0, 'tile', inner)  1.92 us
    pallas_call x1, Pallas kernels, heights_and_state(): pl.pallas_call(height_kernel, in_specs=[SMEM] + [VMEM] * 8, out_specs=[VM...  1.68 us
    unnamed x15, local copies, waits for them, and re-layouts  1.62 us
  transfers between devices with their start and end apart: 5, of which 3 were waited for; matrix products, arithmetic and copies ran while one was open for 0% of the time, Pallas kernels for 2%

profile of v6, /device:TPU:8, one launch (start us, length us, event | category | flops | bytes accessed | tf_op | source)
XLA Modules:
  0.0 49.3 jit_solution(10435772349139955790)
XLA Ops:
  0.6 0.0 copy-start.6
  0.6 0.0 copy-start.3
  0.7 0.0 copy-start.4
  0.7 0.0 copy-start.5
  0.7 0.0 copy-start.2
  0.7 0.0 copy-start.1
  0.7 2.9 %shard_map.121.after_ref = f32[8,64,128]{2,1,0:T(8,128)} custom-call(s32[1,1,8,12]{3,2,1,0:T(8,128)} %src_hbm.1, s32[1,1,8,12]{3,2,1,0:T(8,128)} %cnt_hbm.1, bf16[8,1024]{1,0:T(8,128)(2,1)} %bitcast.27, bf16[8,12,128,128]{3,2,1,0:T(8,128)(2,1)} %bitcast.26), custom_call_target="tpu_custom_call" | custom-call | tf_op jit(solution)/shard_map/pallas_call | solution.py:106
  3.6 14.3 %all-to-all-start = ((f32[8,64,128]{2,1,0:T(8,128)}), f32[8,64,128]{2,1,0:T(8,128)S(1)}, u32[]{:S(2)}, u32[]{:S(2)}) async-start(f32[8,64,128]{2,1,0:T(8,128)} %shard_map.121.after_ref), calls=%async_computation | async-start | bytes 524288 | tf_op jit(solution)/shard_map/all_to_all | solution.py:31
  17.9 0.0 copy-done.6
  17.9 0.0 copy-start
  17.9 1.0 %copy-done = f32[8,64,128]{2,1,0:T(8,128)S(1)} copy-done((f32[8,64,128]{2,1,0:T(8,128)S(1)}, f32[8,64,128]{2,1,0:T(8,128)}, u32[]{:S(2)}) %copy-start) | copy-done | bytes 262168
  18.9 0.2 shard_map.122.onehot_ref
  19.1 4.9 %all-to-all-done.arrived_ref = f32[8,64,128]{2,1,0:T(8,128)S(1)} async-done(((f32[8,64,128]{2,1,0:T(8,128)}), f32[8,64,128]{2,1,0:T(8,128)S(1)}, u32[]{:S(2)}, u32[]{:S(2)}) %all-to-all-start) | async-done | bytes 262176 | tf_op jit(solution)/shard_map/all_to_all | solution.py:31
  24.0 0.0 copy-done.3
  24.0 0.0 copy-done.4
  24.0 0.2 shard_map.123
  24.2 1.9 %collective-permute-start = (f32[32,128]{1,0:T(8,128)S(1)}, f32[32,128]{1,0:T(8,128)S(1)}, u32[]{:S(2)}, u32[]{:S(2)}) collective-permute-start(f32[32,128]{1,0:T(8,128)S(1)} %get-tuple-element.11), channel_id=1, source_target_pairs={{0,1},{1,0},{2,3},{3,2},{4,5},{5,4},{6,7},{7,6},{8,9},{9,8},{10,11... | collective-permute-start | bytes 49160 | tf_op jit(solution)/shard_map/ppermute | solution.py:353
  26.1 9.4 %collective-permute-start.1 = (f32[32,128]{1,0:T(8,128)S(1)}, f32[32,128]{1,0:T(8,128)S(1)}, u32[]{:S(2)}, u32[]{:S(2)}) collective-permute-start(f32[32,128]{1,0:T(8,128)S(1)} %get-tuple-element.12), channel_id=1, source_target_pairs={{0,95},{1,2},{2,1},{3,4},{4,3},{5,6},{6,5},{7,8},{8,7},{9,10},{10,... | collective-permute-start | bytes 49160 | tf_op jit(solution)/shard_map/ppermute | solution.py:354
  35.5 0.7 %collective-permute-start.2 = (f32[32,128]{1,0:T(8,128)S(1)}, f32[32,128]{1,0:T(8,128)S(1)}, u32[]{:S(2)}, u32[]{:S(2)}) collective-permute-start(f32[32,128]{1,0:T(8,128)S(1)} %get-tuple-element.13), channel_id=1, source_target_pairs={{22,23},{23,22},{46,47},{47,46},{70,71},{71,70},{94,95},{95,94},{1... | collective-permute-start | bytes 49160 | tf_op jit(solution)/shard_map/ppermute | solution.py:355
  36.2 0.0 copy-done.5
  36.2 0.0 copy-done.2
  36.2 0.0 copy-done.1
  36.2 0.1 shard_map.124.top_ref
  36.3 0.0 collective-permute-done.got0_ref
  36.3 0.6 %collective-permute-done.1.got1_ref = f32[32,128]{1,0:T(8,128)S(1)} collective-permute-done((f32[32,128]{1,0:T(8,128)S(1)}, f32[32,128]{1,0:T(8,128)S(1)}, u32[]{:S(2)}, u32[]{:S(2)}) %collective-permute-start.1) | collective-permute-done | bytes 16416 | tf_op jit(solution)/shard_map/ppermute | solution.py:354
  36.9 0.0 collective-permute-done.2.got2_ref
  36.9 1.7 %shard_map.125 = (f32[8,128]{1,0:T(8,128)S(1)}, f32[8,3,128]{2,1,0:T(4,128)}) custom-call(s32[1]{0:T(128)} %bitcast.place_ref, f32[32,128]{1,0:T(8,128)S(1)} %collective-permute-done.got0_ref, f32[32,128]{1,0:T(8,128)S(1)} %collective-permute-done.1.got1_ref, f32[32,128]{1,0:T(8,128)S(1)} %collective-permute-done.2.got2_ref, f32[8,128]{1,0:T(8,128)S(1)} %bitcast.22, ...), custom_call_target="tpu_custom_call" | custom-call | tf_op jit(solution)/shard_map/pallas_call | solution.py:317
  38.6 6.7 %all-to-all-start.1 = ((f32[8,3,128]{2,1,0:T(4,128)}), f32[8,3,128]{2,1,0:T(4,128)S(1)}, u32[]{:S(2)}, u32[]{:S(2)}) async-start(f32[8,3,128]{2,1,0:T(4,128)} %get-tuple-element.18), calls=%async_computation.1 | async-start | bytes 32768 | tf_op jit(solution)/shard_map/all_to_all | solution.py:31
  45.3 0.9 %shard_map.126 = (f32[48,1024]{1,0:T(8,128)}, f32[8,128]{1,0:T(8,128)}) custom-call(f32[8,128]{1,0:T(8,128)S(1)} %get-tuple-element.15.height_ref, f32[48,1024]{1,0:T(8,128)S(1)} %bitcast.16, f32[47,8,128]{2,1,0:T(8,128)S(1)} %bitcast.18, f32[40,128]{1,0:T(8,128)S(1)} %get-tuple-element.14.forcing_ref), custom_call_target="tpu_custom_call" | custom-call | flops 4194304 | bytes 4194304 | tf_op jit(solution)/shard_map/pallas_call | solution.py:263
  46.2 2.5 %all-to-all-done.1 = f32[8,3,128]{2,1,0:T(4,128)S(1)} async-done(((f32[8,3,128]{2,1,0:T(4,128)}), f32[8,3,128]{2,1,0:T(4,128)S(1)}, u32[]{:S(2)}, u32[]{:S(2)}) %all-to-all-start.1) | async-done | bytes 12320 | tf_op jit(solution)/shard_map/all_to_all | solution.py:31
  48.7 0.6 %copy.13 = f32[1,1,3,1024]{3,1,2,0:T(1,128)} copy(f32[1,1,3,1024]{3,2,1,0:T(4,128)S(1)} %maximum_bitcast_fusion) | data formatting | bytes 24576
  (2 shorter events, 0.0 us)
Async XLA Ops:
  0.6 17.3 %copy-start.6 = (s32[1,1,8,12]{3,2,1,0:T(8,128)S(1)}, s32[1,1,8,12]{3,2,1,0:T(8,128)}, u32[]{:S(2)}) copy-start(s32[1,1,8,12]{3,2,1,0:T(8,128)} %param.13) | copy-start | bytes 1156
  0.6 23.3 %copy-start.3 = (s32[1,1,6,1024]{3,1,2,0:T(1,128)S(1)}, s32[1,1,6,1024]{3,1,2,0:T(1,128)}, u32[]{:S(2)}) copy-start(s32[1,1,6,1024]{3,1,2,0:T(1,128)} %param.18) | copy-start | bytes 73732
  0.7 23.3 %copy-start.4 = (f32[1,1,1024]{2,1,0:T(1,128)S(1)}, f32[1,1,1024]{2,1,0:T(1,128)}, u32[]{:S(2)}) copy-start(f32[1,1,1024]{2,1,0:T(1,128)} %param.17) | copy-start | bytes 12292
  0.7 35.5 %copy-start.5 = (s32[1,1,1024]{2,1,0:T(1,128)S(1)}, s32[1,1,1024]{2,1,0:T(1,128)}, u32[]{:S(2)}) copy-start(s32[1,1,1024]{2,1,0:T(1,128)} %param.19) | copy-start | bytes 12292
  0.7 35.5 %copy-start.2 = (f32[1,1,47,1024]{3,1,2,0:T(1,128)S(1)}, f32[1,1,47,1024]{3,1,2,0:T(1,128)}, u32[]{:S(2)}) copy-start(f32[1,1,47,1024]{3,1,2,0:T(1,128)} %param.16) | copy-start | bytes 577540
  0.7 35.5 %copy-start.1 = (f32[1,1,48,1024]{3,2,1,0:T(8,128)S(1)}, f32[1,1,48,1024]{3,2,1,0:T(8,128)}, u32[]{:S(2)}) copy-start(f32[1,1,48,1024]{3,2,1,0:T(8,128)} %param.15) | copy-start | bytes 589828
  3.6 20.3 %all-to-all-start = ((f32[8,64,128]{2,1,0:T(8,128)}), f32[8,64,128]{2,1,0:T(8,128)S(1)}, u32[]{:S(2)}, u32[]{:S(2)}) async-start(f32[8,64,128]{2,1,0:T(8,128)} %shard_map.121.after_ref), calls=%async_computation | async-start | bytes 524288 | tf_op jit(solution)/shard_map/all_to_all | solution.py:31
  17.9 1.0 %copy-start = (f32[8,64,128]{2,1,0:T(8,128)S(1)}, f32[8,64,128]{2,1,0:T(8,128)}, u32[]{:S(2)}) copy-start(f32[8,64,128]{2,1,0:T(8,128)} %shard_map.121.after_ref) | copy-start | bytes 786436
  24.2 12.1 %collective-permute-start = (f32[32,128]{1,0:T(8,128)S(1)}, f32[32,128]{1,0:T(8,128)S(1)}, u32[]{:S(2)}, u32[]{:S(2)}) collective-permute-start(f32[32,128]{1,0:T(8,128)S(1)} %get-tuple-element.11), channel_id=1, source_target_pairs={{0,1},{1,0},{2,3},{3,2},{4,5},{5,4},{6,7},{7,6},{8,9},{9,8},{10,11... | collective-permute-start | bytes 49160 | tf_op jit(solution)/shard_map/ppermute | solution.py:353
  26.1 10.8 %collective-permute-start.1 = (f32[32,128]{1,0:T(8,128)S(1)}, f32[32,128]{1,0:T(8,128)S(1)}, u32[]{:S(2)}, u32[]{:S(2)}) collective-permute-start(f32[32,128]{1,0:T(8,128)S(1)} %get-tuple-element.12), channel_id=1, source_target_pairs={{0,95},{1,2},{2,1},{3,4},{4,3},{5,6},{6,5},{7,8},{8,7},{9,10},{10,... | collective-permute-start | bytes 49160 | tf_op jit(solution)/shard_map/ppermute | solution.py:354
  35.5 1.4 %collective-permute-start.2 = (f32[32,128]{1,0:T(8,128)S(1)}, f32[32,128]{1,0:T(8,128)S(1)}, u32[]{:S(2)}, u32[]{:S(2)}) collective-permute-start(f32[32,128]{1,0:T(8,128)S(1)} %get-tuple-element.13), channel_id=1, source_target_pairs={{22,23},{23,22},{46,47},{47,46},{70,71},{71,70},{94,95},{95,94},{1... | collective-permute-start | bytes 49160 | tf_op jit(solution)/shard_map/ppermute | solution.py:355
  38.6 10.1 %all-to-all-start.1 = ((f32[8,3,128]{2,1,0:T(4,128)}), f32[8,3,128]{2,1,0:T(4,128)S(1)}, u32[]{:S(2)}, u32[]{:S(2)}) async-start(f32[8,3,128]{2,1,0:T(4,128)} %get-tuple-element.18), calls=%async_computation.1 | async-start | bytes 32768 | tf_op jit(solution)/shard_map/all_to_all | solution.py:31

commit v7 on v6

--- a/solution.py
+++ b/solution.py
@@ -13,7 +13,7 @@
 LANES = 128
 FIELDS = 5
 TERMS_FIRST = 6
-STATE_FIRST = 4
+STATE_FIRST = 5
 
 heat_gain = 0.5
 shortwave_gain = 0.5

time: 49.7 us -> 49.6 us (level)
  the two profiles are of different devices: /device:TPU:8 before, /device:TPU:40 now
where the time goes in v7:
time: 49.6 us; the launch traced here: 49.3 us
  starting transfers between devices  26.8 us (54%)
  waiting for transfers between devices  14.1 us (28%)
  Pallas kernels  5.97 us (12%)
  local copies, waits for them, and re-layouts  1.62 us (3%)
  between operations  0.77 us (2%)
    all_to_all x2, starting transfers between devices, over_groups(): lax.all_to_all(x, 'comp', split_axis=0, concat_axis=0, axis_index_groups=...  16.9 us
    all_to_all x2, waiting for transfers between devices, over_groups(): lax.all_to_all(x, 'comp', split_axis=0, concat_axis=0, axis_index_groups=...  13.5 us
    ppermute x1, starting transfers between devices, per_device(): got1 = lax.ppermute(pay1, 'tile', outer)  7.33 us
    pallas_call x1, Pallas kernels, remap_terms(): pl.pallas_call(terms_kernel, in_specs=[ANY] * 4, out_specs=ANY, out_shape...  2.91 us
    ppermute x1, starting transfers between devices, per_device(): got0 = lax.ppermute(pay0, 'tile', inner)  1.92 us
    pallas_call x1, Pallas kernels, heights_and_state(): pl.pallas_call(height_kernel, in_specs=[SMEM] + [VMEM] * 8, out_specs=[VM...  1.67 us
    unnamed x15, local copies, waits for them, and re-layouts  1.62 us
  transfers between devices with their start and end apart: 5, of which 3 were waited for; matrix products, arithmetic and copies ran while one was open for 0% of the time, Pallas kernels for 2%

profile of v7, /device:TPU:40, one launch (start us, length us, event | category | flops | bytes accessed | tf_op | source)
XLA Modules:
  0.0 49.3 jit_solution(7290352614347633838)
XLA Ops:
  0.6 0.0 copy-start.6
  0.6 0.0 copy-start.3
  0.7 0.0 copy-start.4
  0.7 0.0 copy-start.5
  0.7 0.0 copy-start.2
  0.7 0.0 copy-start.1
  0.7 2.9 %shard_map.121.after_ref = f32[8,64,128]{2,1,0:T(8,128)} custom-call(s32[1,1,8,12]{3,2,1,0:T(8,128)} %src_hbm.1, s32[1,1,8,12]{3,2,1,0:T(8,128)} %cnt_hbm.1, bf16[8,1024]{1,0:T(8,128)(2,1)} %bitcast.27, bf16[8,12,128,128]{3,2,1,0:T(8,128)(2,1)} %bitcast.26), custom_call_target="tpu_custom_call" | custom-call | tf_op jit(solution)/shard_map/pallas_call | solution.py:106
  3.6 10.9 %all-to-all-start = ((f32[8,64,128]{2,1,0:T(8,128)}), f32[8,64,128]{2,1,0:T(8,128)S(1)}, u32[]{:S(2)}, u32[]{:S(2)}) async-start(f32[8,64,128]{2,1,0:T(8,128)} %shard_map.121.after_ref), calls=%async_computation | async-start | bytes 524288 | tf_op jit(solution)/shard_map/all_to_all | solution.py:31
  14.5 0.0 copy-done.6
  14.5 0.0 copy-start
  14.5 1.0 %copy-done = f32[8,64,128]{2,1,0:T(8,128)S(1)} copy-done((f32[8,64,128]{2,1,0:T(8,128)S(1)}, f32[8,64,128]{2,1,0:T(8,128)}, u32[]{:S(2)}) %copy-start) | copy-done | bytes 262168
  15.5 0.2 shard_map.122.onehot_ref
  15.6 6.6 %all-to-all-done.arrived_ref = f32[8,64,128]{2,1,0:T(8,128)S(1)} async-done(((f32[8,64,128]{2,1,0:T(8,128)}), f32[8,64,128]{2,1,0:T(8,128)S(1)}, u32[]{:S(2)}, u32[]{:S(2)}) %all-to-all-start) | async-done | bytes 262176 | tf_op jit(solution)/shard_map/all_to_all | solution.py:31
  22.2 0.0 copy-done.3
  22.2 0.0 copy-done.4
  22.2 0.2 shard_map.123
  22.4 1.9 %collective-permute-start = (f32[32,128]{1,0:T(8,128)S(1)}, f32[32,128]{1,0:T(8,128)S(1)}, u32[]{:S(2)}, u32[]{:S(2)}) collective-permute-start(f32[32,128]{1,0:T(8,128)S(1)} %get-tuple-element.11), channel_id=1, source_target_pairs={{0,1},{1,0},{2,3},{3,2},{4,5},{5,4},{6,7},{7,6},{8,9},{9,8},{10,11... | collective-permute-start | bytes 49160 | tf_op jit(solution)/shard_map/ppermute | solution.py:353
  24.4 7.3 %collective-permute-start.1 = (f32[32,128]{1,0:T(8,128)S(1)}, f32[32,128]{1,0:T(8,128)S(1)}, u32[]{:S(2)}, u32[]{:S(2)}) collective-permute-start(f32[32,128]{1,0:T(8,128)S(1)} %get-tuple-element.12), channel_id=1, source_target_pairs={{0,95},{1,2},{2,1},{3,4},{4,3},{5,6},{6,5},{7,8},{8,7},{9,10},{10,... | collective-permute-start | bytes 49160 | tf_op jit(solution)/shard_map/ppermute | solution.py:354
  31.7 0.7 %collective-permute-start.2 = (f32[32,128]{1,0:T(8,128)S(1)}, f32[32,128]{1,0:T(8,128)S(1)}, u32[]{:S(2)}, u32[]{:S(2)}) collective-permute-start(f32[32,128]{1,0:T(8,128)S(1)} %get-tuple-element.13), channel_id=1, source_target_pairs={{22,23},{23,22},{46,47},{47,46},{70,71},{71,70},{94,95},{95,94},{1... | collective-permute-start | bytes 49160 | tf_op jit(solution)/shard_map/ppermute | solution.py:355
  32.4 0.0 copy-done.5
  32.4 0.0 copy-done.2
  32.4 0.0 copy-done.1
  32.4 0.1 shard_map.124.top_ref
  32.5 0.0 collective-permute-done.got0_ref
  32.5 0.6 %collective-permute-done.1.got1_ref = f32[32,128]{1,0:T(8,128)S(1)} collective-permute-done((f32[32,128]{1,0:T(8,128)S(1)}, f32[32,128]{1,0:T(8,128)S(1)}, u32[]{:S(2)}, u32[]{:S(2)}) %collective-permute-start.1) | collective-permute-done | bytes 16416 | tf_op jit(solution)/shard_map/ppermute | solution.py:354
  33.1 0.0 collective-permute-done.2.got2_ref
  33.1 1.7 %shard_map.125 = (f32[8,128]{1,0:T(8,128)S(1)}, f32[8,3,128]{2,1,0:T(4,128)}) custom-call(s32[1]{0:T(128)} %bitcast.place_ref, f32[32,128]{1,0:T(8,128)S(1)} %collective-permute-done.got0_ref, f32[32,128]{1,0:T(8,128)S(1)} %collective-permute-done.1.got1_ref, f32[32,128]{1,0:T(8,128)S(1)} %collective-permute-done.2.got2_ref, f32[8,128]{1,0:T(8,128)S(1)} %bitcast.22, ...), custom_call_target="tpu_custom_call" | custom-call | tf_op jit(solution)/shard_map/pallas_call | solution.py:317
  34.8 6.1 %all-to-all-start.1 = ((f32[8,3,128]{2,1,0:T(4,128)}), f32[8,3,128]{2,1,0:T(4,128)S(1)}, u32[]{:S(2)}, u32[]{:S(2)}) async-start(f32[8,3,128]{2,1,0:T(4,128)} %get-tuple-element.18), calls=%async_computation.1 | async-start | bytes 32768 | tf_op jit(solution)/shard_map/all_to_all | solution.py:31
  40.9 0.9 %shard_map.126 = (f32[48,1024]{1,0:T(8,128)}, f32[8,128]{1,0:T(8,128)}) custom-call(f32[8,128]{1,0:T(8,128)S(1)} %get-tuple-element.15.height_ref, f32[48,1024]{1,0:T(8,128)S(1)} %bitcast.16, f32[47,8,128]{2,1,0:T(8,128)S(1)} %bitcast.18, f32[40,128]{1,0:T(8,128)S(1)} %get-tuple-element.14.forcing_ref), custom_call_target="tpu_custom_call" | custom-call | flops 4194304 | bytes 4194304 | tf_op jit(solution)/shard_map/pallas_call | solution.py:263
  41.8 6.9 %all-to-all-done.1 = f32[8,3,128]{2,1,0:T(4,128)S(1)} async-done(((f32[8,3,128]{2,1,0:T(4,128)}), f32[8,3,128]{2,1,0:T(4,128)S(1)}, u32[]{:S(2)}, u32[]{:S(2)}) %all-to-all-start.1) | async-done | bytes 12320 | tf_op jit(solution)/shard_map/all_to_all | solution.py:31
  48.7 0.6 %copy.13 = f32[1,1,3,1024]{3,1,2,0:T(1,128)} copy(f32[1,1,3,1024]{3,2,1,0:T(4,128)S(1)} %maximum_bitcast_fusion) | data formatting | bytes 24576
  (3 shorter events, 0.0 us)
Async XLA Ops:
  0.6 13.8 %copy-start.6 = (s32[1,1,8,12]{3,2,1,0:T(8,128)S(1)}, s32[1,1,8,12]{3,2,1,0:T(8,128)}, u32[]{:S(2)}) copy-start(s32[1,1,8,12]{3,2,1,0:T(8,128)} %param.13) | copy-start | bytes 1156
  0.6 21.6 %copy-start.3 = (s32[1,1,6,1024]{3,1,2,0:T(1,128)S(1)}, s32[1,1,6,1024]{3,1,2,0:T(1,128)}, u32[]{:S(2)}) copy-start(s32[1,1,6,1024]{3,1,2,0:T(1,128)} %param.18) | copy-start | bytes 73732
  0.7 21.5 %copy-start.4 = (f32[1,1,1024]{2,1,0:T(1,128)S(1)}, f32[1,1,1024]{2,1,0:T(1,128)}, u32[]{:S(2)}) copy-start(f32[1,1,1024]{2,1,0:T(1,128)} %param.17) | copy-start | bytes 12292
  0.7 31.7 %copy-start.5 = (s32[1,1,1024]{2,1,0:T(1,128)S(1)}, s32[1,1,1024]{2,1,0:T(1,128)}, u32[]{:S(2)}) copy-start(s32[1,1,1024]{2,1,0:T(1,128)} %param.19) | copy-start | bytes 12292
  0.7 31.7 %copy-start.2 = (f32[1,1,47,1024]{3,1,2,0:T(1,128)S(1)}, f32[1,1,47,1024]{3,1,2,0:T(1,128)}, u32[]{:S(2)}) copy-start(f32[1,1,47,1024]{3,1,2,0:T(1,128)} %param.16) | copy-start | bytes 577540
  0.7 31.7 %copy-start.1 = (f32[1,1,48,1024]{3,2,1,0:T(8,128)S(1)}, f32[1,1,48,1024]{3,2,1,0:T(8,128)}, u32[]{:S(2)}) copy-start(f32[1,1,48,1024]{3,2,1,0:T(8,128)} %param.15) | copy-start | bytes 589828
  3.6 18.6 %all-to-all-start = ((f32[8,64,128]{2,1,0:T(8,128)}), f32[8,64,128]{2,1,0:T(8,128)S(1)}, u32[]{:S(2)}, u32[]{:S(2)}) async-start(f32[8,64,128]{2,1,0:T(8,128)} %shard_map.121.after_ref), calls=%async_computation | async-start | bytes 524288 | tf_op jit(solution)/shard_map/all_to_all | solution.py:31
  14.5 1.0 %copy-start = (f32[8,64,128]{2,1,0:T(8,128)S(1)}, f32[8,64,128]{2,1,0:T(8,128)}, u32[]{:S(2)}) copy-start(f32[8,64,128]{2,1,0:T(8,128)} %shard_map.121.after_ref) | copy-start | bytes 786436
  22.4 10.1 %collective-permute-start = (f32[32,128]{1,0:T(8,128)S(1)}, f32[32,128]{1,0:T(8,128)S(1)}, u32[]{:S(2)}, u32[]{:S(2)}) collective-permute-start(f32[32,128]{1,0:T(8,128)S(1)} %get-tuple-element.11), channel_id=1, source_target_pairs={{0,1},{1,0},{2,3},{3,2},{4,5},{5,4},{6,7},{7,6},{8,9},{9,8},{10,11... | collective-permute-start | bytes 49160 | tf_op jit(solution)/shard_map/ppermute | solution.py:353
  24.4 8.8 %collective-permute-start.1 = (f32[32,128]{1,0:T(8,128)S(1)}, f32[32,128]{1,0:T(8,128)S(1)}, u32[]{:S(2)}, u32[]{:S(2)}) collective-permute-start(f32[32,128]{1,0:T(8,128)S(1)} %get-tuple-element.12), channel_id=1, source_target_pairs={{0,95},{1,2},{2,1},{3,4},{4,3},{5,6},{6,5},{7,8},{8,7},{9,10},{10,... | collective-permute-start | bytes 49160 | tf_op jit(solution)/shard_map/ppermute | solution.py:354
  31.7 1.4 %collective-permute-start.2 = (f32[32,128]{1,0:T(8,128)S(1)}, f32[32,128]{1,0:T(8,128)S(1)}, u32[]{:S(2)}, u32[]{:S(2)}) collective-permute-start(f32[32,128]{1,0:T(8,128)S(1)} %get-tuple-element.13), channel_id=1, source_target_pairs={{22,23},{23,22},{46,47},{47,46},{70,71},{71,70},{94,95},{95,94},{1... | collective-permute-start | bytes 49160 | tf_op jit(solution)/shard_map/ppermute | solution.py:355
  34.8 13.8 %all-to-all-start.1 = ((f32[8,3,128]{2,1,0:T(4,128)}), f32[8,3,128]{2,1,0:T(4,128)S(1)}, u32[]{:S(2)}, u32[]{:S(2)}) async-start(f32[8,3,128]{2,1,0:T(4,128)} %get-tuple-element.18), calls=%async_computation.1 | async-start | bytes 32768 | tf_op jit(solution)/shard_map/all_to_all | solution.py:31
